TPU v7x, 128 devices: a whole 4x4x4 slice. The times are simulated.
128 devices in a mesh: dp: 8 (over z_lo, x), fsdp: 16 (over z_hi, y, core).
Axes of the slice: x: 4, y: 4, z: 4 (z_hi: 2, z_lo: 2; z = z_hi * 2 + z_lo), core: 2. Of those that a mesh axis runs over, the one named last changes fastest.
Arguments:
- activations: bfloat16 [65536, 8192], P('dp', 'fsdp'), may hold values from -6 to 6
- grad_out: bfloat16 [65536, 1024], P(('dp', 'fsdp')), may hold values from -3 to 3
- base_weight: bfloat16 [8192, 1024], P('fsdp'), may hold values from -0.1875 to 0.1875
- down_param: float32 [16, 8192, 64], P('dp', 'fsdp'), may hold values from -0.0625 to 0.0625
- up_param: float32 [16, 64, 1024], P('dp', None, 'fsdp'), may hold values from -0.1875 to 0.1875
- down_first: float32 [16, 8192, 64], P('dp', 'fsdp'), may hold values from -3 to 3
- down_second: float32 [16, 8192, 64], P('dp', 'fsdp'), may hold values from 0.01 to 1
- up_first: float32 [16, 64, 1024], P('dp', None, 'fsdp'), may hold values from -3 to 3
- up_second: float32 [16, 64, 1024], P('dp', None, 'fsdp'), may hold values from 0.01 to 1
- counts: int32 [16], replicated, may hold values from 1 to 7936, 63488 in all
- slot_language: int32 [16], replicated, may hold values from 0 to 15, each once
Outputs:
- input_gradient: bfloat16 [65536, 8192], P('dp', 'fsdp')
- new_down: float32 [16, 8192, 64], P('dp', 'fsdp')
- new_up: float32 [16, 64, 1024], P('dp', None, 'fsdp')
- new_down_first: float32 [16, 8192, 64], P('dp', 'fsdp')
- new_down_second: float32 [16, 8192, 64], P('dp', 'fsdp')
- new_up_first: float32 [16, 64, 1024], P('dp', None, 'fsdp')
- new_up_second: float32 [16, 64, 1024], P('dp', None, 'fsdp')
Inputs may be any that keep to these rules, and one draw needn't show every extreme that they name: Every language has at least one token; the counts sum to (64 * 8 - 16) * 128 and the largest is exactly that over 8. `slot_language`: a permutation: each language in exactly one slot.
All inputs are finite; a program needn't handle non-finite values.
Results may differ from a plain program's by a relative error of at most 0.0055.
Values may be sent and summed in bfloat16 or wider, within the bound.
A program may use at most 128 MiB of HBM per device.

v0:
```python
import jax
import jax.numpy as jnp
from jax import lax
from jax.sharding import PartitionSpec as P

BLK = 128
STEP = 100
BLOCKS_DP = 64


adapter_scale = 2.0
beta_first = 0.9
beta_second = 0.999
learn_rate = 0.001
adam_epsilon = 1e-08


def block_layout(counts, slot_language, first_block, block_total):
    block_count = (counts + BLK - 1) // BLK
    block_start = jnp.cumsum(block_count) - block_count
    block_index = first_block + jnp.arange(block_total, dtype=jnp.int32)
    language = jnp.sum((block_start[None, :] <= block_index[:, None]).astype(jnp.int32), axis=1) - 1
    lang_hot = language[:, None] == jnp.arange(counts.shape[0], dtype=jnp.int32)[None, :]
    lang_start = jnp.sum(jnp.where(lang_hot, block_start[None, :], 0), axis=1)
    lang_count = jnp.sum(jnp.where(lang_hot, counts[None, :], 0), axis=1)
    offset_rows = (block_index - lang_start) * BLK
    live_mask = (
        offset_rows[:, None] + jnp.arange(BLK, dtype=jnp.int32)[None, :] < lang_count[:, None]
    )
    slot_hot = slot_language[None, :] == language[:, None]
    slot_pick = jnp.sum(
        jnp.where(slot_hot, jnp.arange(counts.shape[0], dtype=jnp.int32)[None, :], 0), axis=1
    )
    return (live_mask, slot_pick, slot_hot)


def adam_update(param, first, second, gradient):
    new_first = beta_first * first + (1.0 - beta_first) * gradient
    new_second = beta_second * second + (1.0 - beta_second) * gradient * gradient
    first_hat = new_first / (1.0 - beta_first**STEP)
    second_hat = new_second / (1.0 - beta_second**STEP)
    new_param = param - learn_rate * first_hat / (jnp.sqrt(second_hat) + adam_epsilon)
    return (new_param, new_first, new_second)


def on_device(
    activations,
    grad_out,
    base_weight,
    down_param,
    up_param,
    down_first,
    down_second,
    up_first,
    up_second,
    counts,
    slot_language,
):
    language_group_rows, feature_shard = activations.shape
    rank_width = down_param.shape[2]
    key_local = up_param.shape[2]
    first_block = lax.axis_index("dp") * BLOCKS_DP
    live_mask, slot_pick, slot_hot = block_layout(counts, slot_language, first_block, BLOCKS_DP)
    down_all, up_all = (
        lax.all_gather(down_param.astype(jnp.bfloat16), "dp", axis=0, tiled=True),
        lax.all_gather(up_param.astype(jnp.bfloat16), "dp", axis=0, tiled=True),
    )
    rows_all = lax.all_gather(grad_out, "fsdp", axis=0, tiled=True)
    masked_values = jnp.where(
        live_mask.reshape(language_group_rows)[:, None], rows_all, jnp.zeros((), jnp.bfloat16)
    )
    key_start = lax.axis_index("fsdp") * key_local
    grad_slice = lax.dynamic_slice_in_dim(masked_values, key_start, key_local, 1)
    down_block = jnp.take(down_all, slot_pick, axis=0)
    up_block = jnp.take(up_all, slot_pick, axis=0)
    acts_block = activations.reshape(BLOCKS_DP, BLK, feature_shard)
    grad_block = grad_slice.reshape(BLOCKS_DP, BLK, key_local)
    low_part = jnp.einsum(
        "bnd,bdr->bnr", acts_block, down_block, preferred_element_type=jnp.float32
    )
    back_part = jnp.einsum("bnk,brk->bnr", grad_block, up_block, preferred_element_type=jnp.float32)
    rank_pair = jnp.concatenate([low_part, back_part], axis=2).reshape(
        language_group_rows, 2 * rank_width
    )
    pair_total = lax.psum(rank_pair, "fsdp")
    pair_low = pair_total.astype(jnp.bfloat16)
    pair_low = pair_low.reshape(BLOCKS_DP, BLK, 2 * rank_width)
    reduced_rank_product = pair_low[:, :, :rank_width]
    backward_rank_product = pair_low[:, :, rank_width:]
    frozen_contribution = jnp.einsum(
        "nk,dk->nd", masked_values, base_weight, preferred_element_type=jnp.float32
    )
    adapter_contribution = jnp.einsum(
        "bnr,bdr->bnd", backward_rank_product, down_block, preferred_element_type=jnp.float32
    )
    input_gradient = (
        frozen_contribution
        + adapter_scale * adapter_contribution.reshape(language_group_rows, feature_shard)
    ).astype(jnp.bfloat16)
    down_blockgrad = jnp.einsum(
        "bnd,bnr->bdr", acts_block, backward_rank_product, preferred_element_type=jnp.float32
    )
    up_blockgrad = jnp.einsum(
        "bnr,bnk->brk", reduced_rank_product, grad_block, preferred_element_type=jnp.float32
    )
    slot_float = slot_hot.astype(jnp.float32)
    down_gradient = adapter_scale * jnp.einsum(
        "bs,bdr->sdr", slot_float, down_blockgrad, precision=lax.Precision.HIGHEST
    )
    up_gradient = adapter_scale * jnp.einsum(
        "bs,brk->srk", slot_float, up_blockgrad, precision=lax.Precision.HIGHEST
    )
    down_own, up_own = (
        lax.psum_scatter(down_gradient, "dp", scatter_dimension=0, tiled=True),
        lax.psum_scatter(up_gradient, "dp", scatter_dimension=0, tiled=True),
    )
    new_down, new_down_first, new_down_second = adam_update(
        down_param, down_first, down_second, down_own
    )
    new_up, new_up_first, new_up_second = adam_update(up_param, up_first, up_second, up_own)
    return (
        input_gradient,
        new_down,
        new_up,
        new_down_first,
        new_down_second,
        new_up_first,
        new_up_second,
    )


def solution(mesh):
    placed = (
        P("dp", "fsdp"),
        P(("dp", "fsdp"), None),
        P("fsdp", None),
        P("dp", "fsdp", None),
        P("dp", None, "fsdp"),
        P("dp", "fsdp", None),
        P("dp", "fsdp", None),
        P("dp", None, "fsdp"),
        P("dp", None, "fsdp"),
        P(),
        P(),
    )
    return jax.shard_map(
        on_device,
        mesh=mesh,
        in_specs=placed,
        out_specs=(
            P("dp", "fsdp"),
            P("dp", "fsdp", None),
            P("dp", None, "fsdp"),
            P("dp", "fsdp", None),
            P("dp", "fsdp", None),
            P("dp", None, "fsdp"),
            P("dp", None, "fsdp"),
        ),
        check_vma=False,
    )
```

profile of v0, /device:TPU:1, one launch (start us, length us, event | category | flops | bytes accessed | tf_op | source)
XLA Modules:
  0.0 361.8 jit_solution(7661653782088871436)
XLA Ops:
  7.2 1.7 convert_element_type.17
  11.5 24.7 %all_gather.11 = bf16[16,64,64]{2,1,0:T(8,128)(2,1)S(1)} all-gather(bf16[2,64,64]{2,1,0:T(8,128)(2,1)S(1)} %convert_element_type.18), channel_id=1, replica_groups=mesh['dp'=8,'fsdp'=16] {'dp'}, dimensions={0}, use_global_device_ids=true | all-gather | bytes 147456 | tf_op jit(solution)/shard_map/all_gather | solution.py:66
  37.8 1.7 gather_fusion.1
  39.6 8.1 %all-gather.5.cloned.1.call-done = bf16[16,512,64]{1,2,0:T(8,128)(2,1)} async-done(((bf16[2,512,64]{1,2,0:T(8,128)(2,1)}), bf16[16,512,64]{1,2,0:T(8,128)(2,1)}) %all-gather.5.cloned.1.call-update) | async-done | bytes 1048592 | tf_op jit(solution)/shard_map/all_gather | solution.py:65
  47.7 4.1 %gather_fusion = bf16[64,512,64]{1,2,0:T(8,128)(2,1)} fusion(bf16[16,512,64]{1,2,0:T(8,128)(2,1)} %all-gather.5.cloned.1.call-done, s32[1024]{0:T(1024)S(1)} %pad_clamp_fusion), kind=kCustom, calls=%fused_computation | custom fusion | bytes 8388864 | tf_op jit(solution)/shard_map/jit(_take)/gather | solution.py:74
  51.7 7.7 %fusion.10 = f32[64,128,64]{1,2,0:T(8,128)S(1)} fusion(bf16[64,128,512]{2,1,0:T(8,128)(2,1)} %bitcast.33, bf16[64,512,64]{1,2,0:T(8,128)(2,1)} %gather_fusion, pred[64]{0:T(512)(128)(4,1)S(1)} %compare_and_fusion), kind=kOutput, calls=%fused_computation.18 | convolution fusion | flops 538968064 | bytes 14680128 | tf_op jit(solution)/shard_map/bnd,bdr->bnr/dot_general | solution.py:78
  59.4 105.8 %all-gather.3.cloned.1.call-done = bf16[8192,1024]{1,0:T(8,128)(2,1)} async-done(((bf16[512,1024]{1,0:T(8,128)(2,1)}), bf16[8192,1024]{1,0:T(8,128)(2,1)}) %all-gather.3.cloned.1.call-update) | async-done | bytes 16777232 | tf_op jit(solution)/shard_map/all_gather | solution.py:68
  165.2 8.3 %broadcast_select_fusion = bf16[8192,1024]{1,0:T(8,128)(2,1)S(1)} fusion(bf16[8192,1024]{1,0:T(8,128)(2,1)} %all-gather.3.cloned.1.call-done, pred[8192]{0:T(1024)(128)(4,1)S(1)} %fusion.23), kind=kLoop, calls=%fused_computation.4 | loop fusion | flops 8388608 | bytes 33562624 | tf_op jit(solution)/shard_map/jit(_where)/select_n | solution.py:69
  173.6 5.7 %copy-done.1 = bf16[8192,1024]{1,0:T(8,128)(2,1)} copy-done((bf16[8192,1024]{1,0:T(8,128)(2,1)}, bf16[8192,1024]{1,0:T(8,128)(2,1)S(1)}, u32[]{:S(2)}) %copy-start.1) | copy-done | bytes 16777240
  180.0 1.4 copy-done.2
  181.4 1.5 fusion.17
  182.8 2.3 pad_maximum_fusion
  185.2 5.6 %copy.51 = f32[64,128,128]{2,1,0:T(8,128)} copy(f32[64,128,128]{1,2,0:T(8,128)} %pad_maximum_fusion) | data formatting | bytes 8388608 | tf_op jit(solution)/shard_map/concatenate | solution.py:82
  190.8 77.6 %all-reduce.1 = bf16[8192,128]{1,0:T(8,128)(2,1)S(1)} all-reduce(f32[8192,128]{1,0:T(8,128)} %bitcast.37), channel_id=1, replica_groups=mesh['dp'=8,'fsdp'=16] {'fsdp'}, use_global_device_ids=true, to_apply=%region_5.6 | all-reduce | flops 1048576 | bytes 6291456 | tf_op jit(solution)/shard_map/psum | solution.py:85
  268.4 2.3 fusion.3
  270.7 2.0 fusion.14
  274.0 5.5 %convolution_bitcast_fusion = f32[64,512,64]{1,2,0:T(8,128)S(1)} fusion(bf16[64,128,512]{2,1,0:T(8,128)(2,1)} %bitcast.34, bf16[64,128,128]{2,1,0:T(8,128)(2,1)S(1)} %bitcast.31), kind=kOutput, calls=%fused_computation.10 | convolution fusion | flops 536870912 | bytes 18874368 | tf_op jit(solution)/shard_map/bnd,bnr->bdr/dot_general | solution.py:100
  279.5 7.8 %fusion.11 = f32[16,512,64]{1,0,2:T(8,128)S(1)} fusion(f32[64,512,64]{1,2,0:T(8,128)S(1)} %convolution_bitcast_fusion, s32[64]{0:T(128)S(1)} %broadcast_add_fusion, s32[16]{0:T(128)S(1)} %copy-done.10), kind=kOutput, calls=%fused_computation.19 | convolution fusion | flops 403178496 | bytes 10486080 | tf_op jit(solution)/shard_map/bs,bdr->sdr/dot_general | solution.py:107
  287.3 2.5 copy.54
  289.8 10.6 %convolution_multiply_fusion = f32[64,128,512]{2,1,0:T(8,128)} fusion(bf16[64,128,128]{2,1,0:T(8,128)(2,1)S(1)} %bitcast.32, bf16[64,512,64]{1,2,0:T(8,128)(2,1)} %gather_fusion, pred[64]{0:T(512)(128)(4,1)S(1)} %compare_and_fusion), kind=kOutput, calls=%fused_computation.5 | convolution fusion | flops 543162368 | bytes 23068736 | tf_op jit(solution)/shard_map/bnr,bdr->bnd/dot_general | solution.py:93
  300.4 19.5 %fusion = bf16[8192,512]{1,0:T(8,128)(2,1)} fusion(f32[64,128,512]{2,1,0:T(8,128)} %convolution_multiply_fusion, bf16[8192,1024]{1,0:T(8,128)(2,1)} %copy-done.1, bf16[512,1024]{1,0:T(8,128)(2,1)S(1)} %copy-done), kind=kOutput, calls=%fused_computation.3 | convolution fusion | flops 8598323200 | bytes 42991616 | tf_op jit(solution)/shard_map/nk,dk->nd/dot_general | solution.py:90
  319.9 1.5 divide_subtract_fusion.1
  321.5 31.8 %reduce-scatter.3.cloned.1.call-done = f32[2,512,64]{1,2,0:T(8,128)} async-done(((f32[16,512,64]{1,2,0:T(8,128)}), f32[2,512,64]{1,2,0:T(8,128)}) %reduce-scatter.3.cloned.1.call-update) | async-done | bytes 262160 | tf_op jit(solution)/shard_map/reduce_scatter | solution.py:114
  353.3 1.9 divide_subtract_fusion
  (46 shorter events, 6.2 us)
Async XLA Ops:
  7.2 293.2 %copy-start = (bf16[512,1024]{1,0:T(8,128)(2,1)S(1)}, bf16[512,1024]{1,0:T(8,128)(2,1)}, u32[]{:S(2)}) copy-start(bf16[512,1024]{1,0:T(8,128)(2,1)} %param.13) | copy-start | bytes 3145732
  7.2 40.5 %all-gather.5.cloned.1.call-start = ((), (), s32[]{:S(2)}) async-start(), calls=%async_computation.3 | async-start | bytes 1179648 | tf_op jit(solution)/shard_map/all_gather | solution.py:65
  9.0 156.3 %all-gather.3.cloned.1.call-start = ((), (), s32[]{:S(2)}) async-start(), calls=%async_computation.2 | async-start | bytes 17825792 | tf_op jit(solution)/shard_map/all_gather | solution.py:68
  9.7 310.2 %reduce-scatter.5.cloned.1.call-start = ((), (), s32[]{:S(2)}) async-start(), calls=%async_computation.5 | async-start | bytes 589824 | tf_op jit(solution)/shard_map/reduce_scatter | solution.py:115
  173.6 5.7 %copy-start.1 = (bf16[8192,1024]{1,0:T(8,128)(2,1)}, bf16[8192,1024]{1,0:T(8,128)(2,1)S(1)}, u32[]{:S(2)}) copy-start(bf16[8192,1024]{1,0:T(8,128)(2,1)S(1)} %broadcast_select_fusion) | copy-start | bytes 50331652
  179.3 2.1 copy-start.3
  180.0 1.4 copy-start.2
  268.4 2.3 copy-start.10
  273.7 79.6 %reduce-scatter.3.cloned.1.call-start = ((), (), s32[]{:S(2)}) async-start(), calls=%async_computation.4 | async-start | bytes 2359296 | tf_op jit(solution)/shard_map/reduce_scatter | solution.py:114
  300.4 19.5 %copy-start.7 = (f32[2,64,64]{2,1,0:T(8,128)S(1)}, f32[2,64,64]{2,1,0:T(8,128)}, u32[]{:S(2)}) copy-start(f32[2,64,64]{2,1,0:T(8,128)} %param.15) | copy-start | bytes 98308
  300.4 19.5 %copy-start.8 = (f32[2,64,64]{2,1,0:T(8,128)S(1)}, f32[2,64,64]{2,1,0:T(8,128)}, u32[]{:S(2)}) copy-start(f32[2,64,64]{2,1,0:T(8,128)} %param.18) | copy-start | bytes 98308
  300.4 19.5 %copy-start.9 = (f32[2,64,64]{2,1,0:T(8,128)S(1)}, f32[2,64,64]{2,1,0:T(8,128)}, u32[]{:S(2)}) copy-start(f32[2,64,64]{2,1,0:T(8,128)} %param.19) | copy-start | bytes 98308
  300.4 52.9 %copy-start.4 = (f32[2,512,64]{1,2,0:T(8,128)S(1)}, f32[2,512,64]{1,2,0:T(8,128)}, u32[]{:S(2)}) copy-start(f32[2,512,64]{1,2,0:T(8,128)} %param.14) | copy-start | bytes 786436
  300.4 52.9 %copy-start.5 = (f32[2,512,64]{1,2,0:T(8,128)S(1)}, f32[2,512,64]{1,2,0:T(8,128)}, u32[]{:S(2)}) copy-start(f32[2,512,64]{1,2,0:T(8,128)} %param.16) | copy-start | bytes 786436
  300.4 52.9 %copy-start.6 = (f32[2,512,64]{1,2,0:T(8,128)S(1)}, f32[2,512,64]{1,2,0:T(8,128)}, u32[]{:S(2)}) copy-start(f32[2,512,64]{1,2,0:T(8,128)} %param.17) | copy-start | bytes 786436
Sparse Core Ops, SparseCore 0:
  10.2 37.3 all-gather.4
  50.1 115.0 all-gather.2
  273.9 35.8 reduce-scatter.4
  312.2 41.0 reduce-scatter.2
where the time goes:
time: 367 us; the launch traced here: 362 us
  waiting for transfers between devices  146 us (40%)
  blocking collectives  102 us (28%)
  matrix products  56.9 us (16%)
  local copies, waits for them, and re-layouts  22.8 us (6%)
  other arithmetic  19.1 us (5%)
  between operations  13.9 us (4%)
    all_gather x1, waiting for transfers between devices, on_device(): rows_all = lax.all_gather(grad_out, 'fsdp', axis=0, tiled=True)  106 us
    psum x1, blocking collectives, on_device(): pair_total = lax.psum(rank_pair, 'fsdp')  77.6 us
    reduce_scatter x1, waiting for transfers between devices, on_device(): lax.psum_scatter(down_gradient, 'dp', scatter_dimension=0, tiled=True)  31.8 us
    all_gather x1, blocking collectives, on_device(): lax.all_gather(up_param.astype(jnp.bfloat16), 'dp', axis=0, tiled=True)  24.7 us
    dot_general x1, matrix products, on_device(): jnp.einsum('nk,dk->nd', masked_values, base_weight, preferred_element_typ...  19.5 us
    dot_general x1, matrix products, on_device(): jnp.einsum('bnr,bdr->bnd', backward_rank_product, down_block, preferred_e...  10.6 us
    select_n x1, other arithmetic, on_device(): jnp.where(live_mask.reshape(language_group_rows)[:, None], rows_all, jnp....  8.33 us
    all_gather x1, waiting for transfers between devices, on_device(): lax.all_gather(down_param.astype(jnp.bfloat16), 'dp', axis=0, tiled=True)  8.06 us
  transfers between devices with their start and end apart: 4, of which 3 were waited for; matrix products, arithmetic and copies ran while one was open for 18% of the time, Pallas kernels for 0%

commit v1 on v0

v1 whole, which is shorter than its diff:
```python
import jax
import jax.numpy as jnp
from jax import lax
from jax.experimental import pallas as pl
from jax.experimental.pallas import tpu as pltpu
from jax.sharding import PartitionSpec as P

BLK = 128
STEP = 100
BLOCKS_DP = 64
LANGS = 16
RANK = 64
ROWS_OWN = 512
FEATURES = 512
KEYS = 1024

adapter_scale = 2.0
beta_first = 0.9
beta_second = 0.999
learn_rate = 0.001
adam_epsilon = 1e-08

MESH = pl.DeviceIdType.MESH
F32 = jnp.float32
BF16 = jnp.bfloat16
LAST = (((1,), (1,)), ((), ()))
FIRST = (((0,), (0,)), ((), ()))
CUT = 144
CHIPS = [(1, 0), (3, 0), (2, 0), (0, 1), (1, 1), (3, 1), (2, 1)]
PLANE = [(dy, dz) for dz in range(4) for dy in range(4) if (dy, dz) != (0, 0)]
DATA = [(dx, dl) for dl in range(2) for dx in range(4) if (dx, dl) != (0, 0)]


def adam_update(param, first, second, gradient):
    new_first = beta_first * first + (1.0 - beta_first) * gradient
    new_second = beta_second * second + (1.0 - beta_second) * gradient * gradient
    first_hat = new_first / (1.0 - beta_first**STEP)
    second_hat = new_second / (1.0 - beta_second**STEP)
    new_param = param - learn_rate * first_hat / (jnp.sqrt(second_hat) + adam_epsilon)
    return (new_param, new_first, new_second)


def block_layout(counts, slot_language, first_block):
    ids = jnp.arange(LANGS, dtype=jnp.int32)
    owner = slot_language[:, None]
    count = jnp.sum(jnp.where(ids[None, :] == owner, counts[None, :], 0), axis=1)
    start = jnp.sum(jnp.where(ids[None, :] < owner, (counts[None, :] + BLK - 1) // BLK, 0), axis=1)
    behind = first_block + jnp.arange(BLOCKS_DP, dtype=jnp.int32)[:, None] - start[None, :]
    left = count[None, :] - behind * BLK
    hot = (behind >= 0) & (left > 0)
    return (
        jnp.sum(jnp.where(hot, ids[None, :], 0), axis=1),
        jnp.sum(jnp.where(hot, left, 0), axis=1),
    )


def kernel(
    slot_ref, left_ref, acts_hbm, grad_hbm, base_hbm, down_hbm, up_hbm,
    out_hbm, down_out, up_out,
    G, ACT, BASE, WT, DOWN, UPOWN, UP, UMINE, USIB, DT, BK, LW, LOWN, LSIB, LGOT, LSUM, LARR,
    DG, DSEND, DARR, DZ, DZARR, UG, USEND, UARR, EXP, OB, send_sems, recv_sems, local_sems, out_sems,
):
    dp, f = lax.axis_index("dp"), lax.axis_index("fsdp")
    x, zl = lax.rem(dp, 4), dp // 4
    c, chip = lax.rem(f, 2), f // 2
    y, h = lax.rem(chip, 4), chip // 4
    z = h * 2 + zl

    def at(dx=0, dy=0, dz=0, dc=0):
        zz = lax.rem(z + dz, 4)
        return (
            lax.rem(zz, 2) * 4 + lax.rem(x + dx, 4),
            (zz // 2) * 8 + lax.rem(y + dy, 4) * 2 + lax.rem(c + dc, 2),
        )

    def flip(dx):
        return ((1 - zl) * 4 + lax.rem(x + dx, 4), f)

    def chip_of(dy, dh):
        return lax.rem(h + dh, 2) * 4 + lax.rem(y + dy, 4)

    makers = {}

    def message(name, src, dst, device):
        k = len(makers)
        makers[name] = lambda: pltpu.make_async_remote_copy(
            src_ref=src(),
            dst_ref=dst(),
            send_sem=send_sems.at[k],
            recv_sem=recv_sems.at[k],
            device_id=device(),
            device_id_type=MESH,
        )

    def same(name, ref, device):
        message(name, ref, ref, device)

    def start(*names):
        for name in names:
            makers[name]().start()

    def got(*names):
        for name in names:
            makers[name]().wait_recv()

    def rows(name, by, bh, lo, hi, **to):
        same(name, lambda: G.at[chip_of(by, bh) * 2 + c, pl.ds(lo, hi - lo)], lambda: at(**to))

    top, low_end, n = CUT, ROWS_OWN - CUT, ROWS_OWN
    half = n // 2
    plus, minus, across, sibling = dict(dy=1), dict(dy=3), dict(dz=2), dict(dc=1)
    rows("yp0", 0, 0, 0, half, **plus)
    rows("ym1", 0, 0, half, n, **minus)
    rows("zA0", 0, 0, 0, top, **across)
    rows("zA1", 0, 0, low_end, n, **across)
    rows("yp1", 0, 0, half, n, **plus)
    rows("ym0", 0, 0, 0, half, **minus)
    rows("zB", 0, 0, top, low_end, **across)
    rows("c0", 0, 0, 0, n, **sibling)
    rows("ap0", 0, 1, 0, top, **plus)
    rows("am0", 0, 1, 0, top, **minus)
    rows("ap1", 0, 1, low_end, n, **plus)
    rows("am1", 0, 1, low_end, n, **minus)
    rows("fp", 3, 0, 0, half, **plus)
    rows("fm", 1, 0, half, n, **minus)
    rows("zBm", 3, 0, top, low_end, **across)
    rows("zBp", 1, 0, top, low_end, **across)
    rows("c1", 3, 0, 0, n, **sibling)
    rows("c2", 1, 0, 0, n, **sibling)
    rows("c3", 0, 1, 0, n, **sibling)
    rows("fap", 3, 1, 0, top, **plus)
    rows("fam", 1, 1, low_end, n, **minus)
    rows("zB2", 2, 0, top, low_end, **across)
    rows("c4", 2, 0, 0, n, **sibling)
    rows("c5", 3, 1, 0, n, **sibling)
    rows("c6", 1, 1, 0, n, **sibling)
    rows("c7", 2, 1, 0, n, **sibling)
    message("u0", lambda: UMINE, lambda: USIB, lambda: at(dc=1))
    for k, (dy, dz) in enumerate(PLANE):
        same(
            f"u1_{k}",
            lambda: UP.at[dp, c, :, pl.ds(pl.multiple_of(chip * 128, 128), 128)],
            lambda dy=dy, dz=dz: at(dy=dy, dz=dz),
        )
    for dx in (1, 3, 2):
        for l in (0, 1):
            same(f"u2_{dx}_{l}", lambda l=l: UP.at[l * 4 + x, c], lambda dx=dx: at(dx=dx))
    same("u3", lambda: UP.at[:, c], lambda: at(dc=1))
    same("d0", lambda: DT.at[pl.ds(dp * 2, 2)], lambda: flip(0))
    for dx in (1, 3, 2):
        for l in (0, 1):
            same(
                f"d1_{dx}_{l}",
                lambda l=l: DT.at[pl.ds(((zl + l) % 2 * 4 + x) * 2, 2)],
                lambda dx=dx: at(dx=dx),
            )
    for k, (dy, dh) in enumerate(CHIPS):
        to = lambda dy=dy, dh=dh: at(dy=dy, dz=2 * dh)
        same(f"b_{k}", lambda: BK.at[chip, c], to)
        message(
            f"l1_{k}", lambda dy=dy, dh=dh: LSUM.at[chip_of(dy, dh)], lambda k=k: LARR.at[k], to
        )
        same(f"l2_{k}", lambda: LW.at[chip, c], to)
    same("b_c", lambda: BK.at[:, c], lambda: at(dc=1))
    same("l2_c", lambda: LW.at[:, c], lambda: at(dc=1))
    message("l0", lambda: LSIB, lambda: LGOT, lambda: at(dc=1))
    for k, dx in enumerate((1, 3, 2)):
        for l in (0, 1):
            message(
                f"r0_{k}_{l}",
                lambda dx=dx, l=l: DSEND.at[pl.ds((l * 4 + lax.rem(x + dx, 4)) * 2, 2)],
                lambda k=k, l=l: DARR.at[k, l],
                lambda dx=dx: at(dx=dx),
            )
    message("r1", lambda: DZ, lambda: DZARR, lambda: flip(0))
    for k, (dx, dl) in enumerate(DATA):
        message(
            f"v_{k}",
            lambda dx=dx, dl=dl: USEND.at[lax.rem(zl + dl, 2) * 4 + lax.rem(x + dx, 4)],
            lambda k=k: UARR.at[k],
            lambda dx=dx, dl=dl: (lax.rem(zl + dl, 2) * 4 + lax.rem(x + dx, 4), f),
        )

    loads = [
        pltpu.make_async_copy(up_hbm, UPOWN, local_sems.at[0]),
        pltpu.make_async_copy(grad_hbm, G.at[f], local_sems.at[1]),
        pltpu.make_async_copy(down_hbm, DOWN, local_sems.at[2]),
        pltpu.make_async_copy(base_hbm, BASE, local_sems.at[3]),
        pltpu.make_async_copy(acts_hbm, ACT, local_sems.at[4]),
    ]
    for load in loads:
        load.start()
    barrier = pltpu.get_barrier_semaphore()
    peers = [at(dy=dy, dz=dz) for dy, dz in PLANE] + [at(dc=1)]
    peers += [at(dx=dx) for dx in (1, 2, 3)] + [flip(dx) for dx in (1, 2, 3)]
    for peer in peers:
        pl.semaphore_signal(barrier, inc=1, device_id=peer, device_id_type=MESH)

    loads[0].wait()
    own_up = UPOWN[...].reshape(2 * RANK, RANK)
    none = jnp.zeros_like(own_up)
    first_core = jnp.where(c == 0, 1.0, 0.0).astype(F32)
    UMINE[...] = (
        jnp.concatenate([own_up, none], axis=1) * first_core
        + jnp.concatenate([none, own_up], axis=1) * (1.0 - first_core)
    ).astype(BF16)
    loads[1].wait()
    for j in range(4):
        inside = lax.broadcasted_iota(jnp.int32, (BLK, KEYS), 0) < left_ref[f * 4 + j]
        part = G[f, pl.ds(j * BLK, BLK)].astype(F32)
        G[f, pl.ds(j * BLK, BLK)] = jnp.where(inside, part, 0.0).astype(BF16)
    pl.semaphore_wait(barrier, len(peers))

    start("u0")
    loads[2].wait()
    for s in range(2):
        DT[dp * 2 + s] = DOWN[s].T.astype(BF16)
    start("d0")
    start("yp0", "ym1", "zA0", "zA1", "yp1", "ym0", "zB", "c0")
    got("u0")
    mine, theirs = UMINE[pl.ds(c * RANK, RANK)], USIB[pl.ds(c * RANK, RANK)]
    UP[dp, c, :, pl.ds(pl.multiple_of(chip * 128, 128), 128)] = (
        mine.astype(F32) + theirs.astype(F32)
    ).astype(BF16)
    start(*[f"u1_{k}" for k in range(len(PLANE))])
    got("d0")
    start(*[f"d1_{dx}_{l}" for dx in (1, 3, 2) for l in (0, 1)])
    got(*[f"u1_{k}" for k in range(len(PLANE))])
    start(*[f"u2_{dx}_{l}" for dx in (1, 3, 2) for l in (0, 1)])
    loads[3].wait()
    WT[...] = BASE[...].T
    got("zA0")
    start("ap0", "am0")
    got("zA1")
    start("ap1", "am1")
    got(*[f"d1_{dx}_{l}" for dx in (1, 3, 2) for l in (0, 1)])
    loads[4].wait()

    def partial_low(fb):
        parts = []
        for j in range(4):
            block = ACT[pl.ds(fb * ROWS_OWN + j * BLK, BLK)]
            parts.append(
                lax.dot_general(DT[slot_ref[fb * 4 + j]], block, LAST, preferred_element_type=F32)
            )
        return jnp.concatenate(parts, axis=1)

    def low_step(q, _):
        @pl.when(q == 2)
        def _():
            got("yp0")
            start("fp")
            got("ym1")
            start("fm")

        LSIB[q] = partial_low(q * 2 + 1 - c).astype(BF16)
        LOWN[q] = partial_low(q * 2 + c)
        return 0

    lax.fori_loop(0, 8, low_step, 0)
    start("l0")
    got("yp1")
    start("zBm", "c1")
    got("ym0")
    start("zBp", "c2")
    got("l0")

    def sum_step(q, _):
        total = LOWN[q] + LGOT[q].astype(F32)
        LOWN[q] = total
        LSUM[q] = total.astype(BF16)
        return 0

    lax.fori_loop(0, 8, sum_step, 0)
    start(*[f"l1_{k}" for k in range(7)])

    got(*[f"u2_{dx}_{l}" for dx in (1, 3, 2) for l in (0, 1)])
    start("u3")
    got("u3")
    for j in range(4):
        s = slot_ref[f * 4 + j]
        BK[chip, c, :, pl.ds(j * BLK, BLK)] = lax.dot_general(
            UP[s // 2, s % 2], G[f, pl.ds(j * BLK, BLK)], LAST, preferred_element_type=F32
        ).astype(BF16)
    start(*[f"b_{k}" for k in range(7)])
    got("zB")
    start("c3")
    got(*[f"l1_{k}" for k in range(7)])
    total = LOWN[chip]
    for k in range(7):
        total += LARR[k].astype(F32)
    LW[chip, c] = total.astype(BF16)
    start(*[f"l2_{k}" for k in range(7)])
    got(*[f"b_{k}" for k in range(7)])
    start("b_c")
    got("ap0")
    start("fap")
    got("am1")
    start("fam")
    got("b_c")

    def spread(source, fb):
        for j in range(4):
            slot = slot_ref[fb * 4 + j]
            part = source[fb // 2, fb % 2, :, pl.ds(j * BLK, BLK)].astype(F32)
            for s in range(LANGS):
                weight = jnp.where(slot == s, 1.0, 0.0).astype(F32)
                EXP[pl.ds(s * RANK, RANK), pl.ds(j * BLK, BLK)] = (part * weight).astype(BF16)

    def down_step(fb, _):
        @pl.when(fb == 6)
        def _():
            got("fp", "fm")
            start("zB2", "c4")

        @pl.when(fb == 10)
        def _():
            got(*[f"l2_{k}" for k in range(7)])
            start("l2_c")

        spread(BK, fb)
        part = jnp.dot(
            EXP[...], ACT[pl.ds(fb * ROWS_OWN, ROWS_OWN)], preferred_element_type=F32
        )

        @pl.when(fb == 0)
        def _():
            DG[...] = part

        @pl.when(fb > 0)
        def _():
            DG[...] += part

        return 0

    lax.fori_loop(0, 16, down_step, 0)

    def scale_step(s, _):
        total = adapter_scale * DG[pl.ds(s * RANK, RANK)]
        DG[pl.ds(s * RANK, RANK)] = total
        DSEND[s] = total.astype(BF16)
        return 0

    lax.fori_loop(0, LANGS, scale_step, 0)
    start(*[f"r0_{k}_{l}" for k in range(3) for l in (0, 1)])
    got("l2_c")

    order = [(0, 0), (3, 0), (1, 0), (0, 1), (2, 0), (3, 1), (1, 1), (2, 1)]

    def write(fb, slot):
        return pltpu.make_async_copy(
            OB.at[slot], out_hbm.at[pl.ds(fb * ROWS_OWN, ROWS_OWN)], out_sems.at[slot]
        )

    def down_sum(l):
        total = DG[pl.ds((l * 4 + x) * 2 * RANK, 2 * RANK)]
        for k in range(3):
            total += DARR[k, l].astype(F32).reshape(2 * RANK, FEATURES)
        return total

    def main_step(t, _):
        i, core = t // 2, t % 2
        dy = jnp.int32(0)
        dh = jnp.int32(0)
        for k, (a, b) in enumerate(order):
            dy = jnp.where(i == k, a, dy)
            dh = jnp.where(i == k, b, dh)
        fb = chip_of(dy, dh) * 2 + lax.rem(c + core, 2)

        @pl.when(t == 1)
        def _():
            got("c0")

        @pl.when(t == 3)
        def _():
            got("c1")

        @pl.when(t == 4)
        def _():
            got("ap1", "zBm")
            start("c5")

        @pl.when(t == 5)
        def _():
            got("c2", "am0", "zBp")
            start("c6")

        @pl.when(t == 7)
        def _():
            got("c3")
            got(*[f"r0_{k}_{l}" for k in range(3) for l in (0, 1)])
            DZ[...] = down_sum(1 - zl).astype(BF16)
            start("r1")

        @pl.when(t == 9)
        def _():
            got("c4")

        @pl.when(t == 11)
        def _():
            got("c5")

        @pl.when(t == 12)
        def _():
            got("fap", "fam", "zB2")
            start("c7")

        @pl.when(t == 13)
        def _():
            got("c6")

        @pl.when(t == 15)
        def _():
            got("c7")

        spread(LW, fb)
        part = jnp.dot(
            EXP[...],
            G[fb, :, pl.ds(pl.multiple_of(chip * 128, 128), 128)],
            preferred_element_type=F32,
        )

        @pl.when(t == 0)
        def _():
            UG[...] = part

        @pl.when(t > 0)
        def _():
            UG[...] += part

        @pl.when(t == 15)
        def _():
            lane = lax.broadcasted_iota(jnp.int32, (RANK, 128), 1)
            for d in range(8):
                even = adapter_scale * UG[pl.ds(d * 2 * RANK, RANK)]
                odd = adapter_scale * UG[pl.ds(d * 2 * RANK + RANK, RANK)]
                left = jnp.where(lane < RANK, even, pltpu.roll(odd, RANK, 1))
                right = jnp.where(lane < RANK, pltpu.roll(even, RANK, 1), odd)
                USEND[d] = left * first_core + right * (1.0 - first_core)
            start(*[f"v_{k}" for k in range(7)])

        slot = t % 2

        @pl.when(t >= 2)
        def _():
            write(fb, slot).wait()

        frozen = jnp.dot(G[fb], WT[...], preferred_element_type=F32)
        for j in range(4):
            low = lax.dot_general(
                BK[fb // 2, fb % 2, :, pl.ds(j * BLK, BLK)],
                DT[slot_ref[fb * 4 + j]],
                FIRST,
                preferred_element_type=F32,
            )
            OB[slot, pl.ds(j * BLK, BLK)] = (
                frozen[j * BLK : (j + 1) * BLK] + adapter_scale * low
            ).astype(BF16)
        write(fb, slot).start()
        return 0

    lax.fori_loop(0, 16, main_step, 0)
    got("r1")
    total = down_sum(zl) + DZARR[...].astype(F32)
    down_out[0] = total[:RANK].T
    down_out[1] = total[RANK:].T
    got(*[f"v_{k}" for k in range(7)])
    total = USEND[dp]
    for k in range(7):
        total += UARR[k]
    up_out[...] = total
    write(f, 0).wait()
    write(f, 1).wait()
    for name in makers:
        makers[name]().wait_send()


def on_device(
    activations,
    grad_out,
    base_weight,
    down_param,
    up_param,
    down_first,
    down_second,
    up_first,
    up_second,
    counts,
    slot_language,
):
    slots, left = block_layout(counts, slot_language, lax.axis_index("dp") * BLOCKS_DP)
    smem = pl.BlockSpec(memory_space=pltpu.SMEM)
    anywhere = pl.BlockSpec(memory_space=pl.ANY)
    vmem = pl.BlockSpec(memory_space=pltpu.VMEM)
    n_messages = 120
    input_gradient, down_own, up_own = pl.pallas_call(
        kernel,
        out_shape=(
            jax.ShapeDtypeStruct(activations.shape, BF16),
            jax.ShapeDtypeStruct((2, FEATURES, RANK), F32),
            jax.ShapeDtypeStruct((RANK, 128), F32),
        ),
        in_specs=[smem, smem] + [anywhere] * 5,
        out_specs=(anywhere, vmem, vmem),
        scratch_shapes=[
            pltpu.VMEM((16, ROWS_OWN, KEYS), BF16),
            pltpu.VMEM((16 * ROWS_OWN, FEATURES), BF16),
            pltpu.VMEM((FEATURES, KEYS), BF16),
            pltpu.VMEM((KEYS, FEATURES), BF16),
            pltpu.VMEM((2, FEATURES, RANK), F32),
            pltpu.VMEM((2, RANK, RANK), F32),
            pltpu.VMEM((8, 2, RANK, KEYS), BF16),
            pltpu.VMEM((2 * RANK, 128), BF16),
            pltpu.VMEM((2 * RANK, 128), BF16),
            pltpu.VMEM((LANGS, RANK, FEATURES), BF16),
            pltpu.VMEM((8, 2, RANK, ROWS_OWN), BF16),
            pltpu.VMEM((8, 2, RANK, ROWS_OWN), BF16),
            pltpu.VMEM((8, RANK, ROWS_OWN), F32),
            pltpu.VMEM((8, RANK, ROWS_OWN), BF16),
            pltpu.VMEM((8, RANK, ROWS_OWN), BF16),
            pltpu.VMEM((8, RANK, ROWS_OWN), BF16),
            pltpu.VMEM((7, RANK, ROWS_OWN), BF16),
            pltpu.VMEM((LANGS * RANK, FEATURES), F32),
            pltpu.VMEM((LANGS, RANK, FEATURES), BF16),
            pltpu.VMEM((3, 2, 2, RANK, FEATURES), BF16),
            pltpu.VMEM((2 * RANK, FEATURES), BF16),
            pltpu.VMEM((2 * RANK, FEATURES), BF16),
            pltpu.VMEM((LANGS * RANK, 128), F32),
            pltpu.VMEM((8, RANK, 128), F32),
            pltpu.VMEM((7, RANK, 128), F32),
            pltpu.VMEM((LANGS * RANK, ROWS_OWN), BF16),
            pltpu.VMEM((2, ROWS_OWN, FEATURES), BF16),
            pltpu.SemaphoreType.DMA((n_messages,)),
            pltpu.SemaphoreType.DMA((n_messages,)),
            pltpu.SemaphoreType.DMA((5,)),
            pltpu.SemaphoreType.DMA((2,)),
        ],
        compiler_params=pltpu.CompilerParams(
            collective_id=0, has_side_effects=True, vmem_limit_bytes=58 * 2**20
        ),
        cost_estimate=pl.CostEstimate(
            flops=2 * 8192 * 512 * 1024 * 3, bytes_accessed=40 * 2**20, transcendentals=0
        ),
    )(slots, left, activations, grad_out, base_weight, down_param, up_param)
    up_gradient = jnp.stack([up_own[:, :RANK], up_own[:, RANK:]])
    new_down, new_down_first, new_down_second = adam_update(
        down_param, down_first, down_second, down_own
    )
    new_up, new_up_first, new_up_second = adam_update(up_param, up_first, up_second, up_gradient)
    return (
        input_gradient,
        new_down,
        new_up,
        new_down_first,
        new_down_second,
        new_up_first,
        new_up_second,
    )


def solution(mesh):
    placed = (
        P("dp", "fsdp"),
        P(("dp", "fsdp"), None),
        P("fsdp", None),
        P("dp", "fsdp", None),
        P("dp", None, "fsdp"),
        P("dp", "fsdp", None),
        P("dp", "fsdp", None),
        P("dp", None, "fsdp"),
        P("dp", None, "fsdp"),
        P(),
        P(),
    )
    return jax.shard_map(
        on_device,
        mesh=mesh,
        in_specs=placed,
        out_specs=(
            P("dp", "fsdp"),
            P("dp", "fsdp", None),
            P("dp", None, "fsdp"),
            P("dp", "fsdp", None),
            P("dp", "fsdp", None),
            P("dp", None, "fsdp"),
            P("dp", None, "fsdp"),
        ),
        check_vma=False,
    )
```

time: 367 us -> 151 us (0.41); the launches traced: 362 us -> 151 us
  waiting for transfers between devices: 146 us -> 0 us
  Pallas kernels: 0 us -> 132 us
  blocking collectives: 102 us -> 0 us
  matrix products: 56.9 us -> 0 us
  other arithmetic: 19.1 us -> 4.23 us
  between operations: 13.9 us -> 0.72 us
  local copies, waits for them, and re-layouts: 22.8 us -> 13.2 us
    pallas_call x0 -> x1, Pallas kernels: none -> 132 us  [on_device(): pl.pallas_call(kernel, out_shape=(jax.ShapeDtypeStruct(activations.shape,...]
    all_gather x2 -> x0, waiting for transfers between devices: 114 us -> none  [the longest x1 106 us: on_device(): rows_all = lax.all_gather(grad_out, 'fsdp', axis=0, tiled=True)]
    psum x1 -> x0, blocking collectives: 77.6 us -> none  [on_device(): pair_total = lax.psum(rank_pair, 'fsdp')]
    dot_general x8 -> x0, matrix products: 56.9 us -> none  [the longest x1 19.5 us: on_device(): jnp.einsum('nk,dk->nd', masked_values, base_weight, preferred_element_typ...]
    reduce_scatter x2 -> x0, waiting for transfers between devices: 31.8 us -> none  [the longest x1 31.8 us: on_device(): lax.psum_scatter(down_gradient, 'dp', scatter_dimension=0, tiled=True)]
    all_gather x1 -> x0, blocking collectives: 24.7 us -> none  [on_device(): lax.all_gather(up_param.astype(jnp.bfloat16), 'dp', axis=0, tiled=True)]
    select_n x2 -> x1, other arithmetic: 8.34 us -> 0.67 us  [block_layout(): (counts[None, :] + BLK - 1) // BLK]
    gather x2 -> x0, local copies, waits for them, and re-layouts: 5.72 us -> none  [the longest x1 4.05 us: on_device(): down_block = jnp.take(down_all, slot_pick, axis=0)]
  transfers between devices with their start and end apart: 4 -> 0, of which waited for: 3 -> 0; matrix products, arithmetic and copies ran while one was open for 18% -> 0% of each run, Pallas kernels for 0% -> 0%
where the time goes in v1:
time: 151 us
  Pallas kernels  132 us (87%)
  local copies, waits for them, and re-layouts  13.2 us (9%)
  other arithmetic  4.23 us (3%)
    pallas_call x1, Pallas kernels, on_device(): pl.pallas_call(kernel, out_shape=(jax.ShapeDtypeStruct(activations.shape,...  132 us
    unnamed x19, local copies, waits for them, and re-layouts  12.3 us

profile of v1, /device:TPU:1, one launch (start us, length us, event | category | flops | bytes accessed | tf_op | source)
XLA Modules:
  0.0 150.5 jit_solution(2640831032511055983)
XLA Ops:
  0.6 0.7 and_select_fusion
  1.3 0.9 select_reduce_fusion.2
  2.2 0.6 fusion.5
  2.8 1.9 %copy.25.down_hbm = f32[2,512,64]{2,1,0:T(8,128)} copy(f32[2,512,64]{1,2,0:T(8,128)} %param.14) | data formatting | bytes 524288 | tf_op args[3]
  4.7 0.0 copy-start.3
  4.7 0.0 copy-start.4
  4.7 0.0 copy-start.2
  4.7 0.0 copy-start
  4.8 132.4 %shard_map.162 = (bf16[8192,512]{1,0:T(8,128)(2,1)}, f32[2,512,64]{2,1,0:T(8,128)}, f32[64,128]{1,0:T(8,128)}) custom-call(s32[64]{0:T(128)} %get-tuple-element.28.slot_ref, s32[64]{0:T(128)} %get-tuple-element.27.left_ref, bf16[8192,512]{1,0:T(8,128)(2,1)} %acts_hbm.1, bf16[512,1024]{1,0:T(8,128)(2,1)} %grad_hbm.1, bf16[512,1024]{1,0:T(8,128)(2,1)} %base_hbm.1, ...), custom_call_target="tpu_custom_call" | custom-call | flops 25769803776 | bytes 41943040 | tf_op jit(solution)/shard_map/pallas_call | solution.py:496
  137.1 0.9 slice_bitcast_fusion.1
  138.0 0.0 copy-done.3
  138.0 0.0 copy-done.4
  138.0 0.0 copy-done.5
  138.0 0.7 divide_subtract_fusion.1
  138.7 0.0 copy-done.1
  138.7 0.2 copy.26
  138.9 0.0 copy-done.2
  139.0 0.2 copy.27
  139.2 0.0 copy-done
  139.2 1.4 divide_subtract_fusion
  140.6 0.9 copy.29
  141.5 0.9 copy.30
  142.3 0.9 copy.31
  143.2 7.3 %copy.33 = bf16[8192,512]{1,0:T(8,128)(2,1)} copy(bf16[8192,512]{1,0:T(8,128)(2,1)} %get-tuple-element.46) | data formatting | bytes 16777216
  (3 shorter events, 0.0 us)
Async XLA Ops:
  4.7 133.3 %copy-start.3 = (f32[2,64,64]{2,1,0:T(8,128)S(1)}, f32[2,64,64]{2,1,0:T(8,128)}, u32[]{:S(2)}) copy-start(f32[2,64,64]{2,1,0:T(8,128)} %up_hbm.1) | copy-start | bytes 98308
  4.7 133.3 %copy-start.4 = (f32[2,64,64]{2,1,0:T(8,128)S(1)}, f32[2,64,64]{2,1,0:T(8,128)}, u32[]{:S(2)}) copy-start(f32[2,64,64]{2,1,0:T(8,128)} %param.18) | copy-start | bytes 98308
  4.7 133.3 %copy-start.5 = (f32[2,64,64]{2,1,0:T(8,128)S(1)}, f32[2,64,64]{2,1,0:T(8,128)}, u32[]{:S(2)}) copy-start(f32[2,64,64]{2,1,0:T(8,128)} %param.19) | copy-start | bytes 98308
  4.7 134.0 %copy-start.1 = (f32[2,512,64]{1,2,0:T(8,128)S(1)}, f32[2,512,64]{1,2,0:T(8,128)}, u32[]{:S(2)}) copy-start(f32[2,512,64]{1,2,0:T(8,128)} %param.16) | copy-start | bytes 786436
  4.7 134.2 %copy-start.2 = (f32[2,512,64]{1,2,0:T(8,128)S(1)}, f32[2,512,64]{1,2,0:T(8,128)}, u32[]{:S(2)}) copy-start(f32[2,512,64]{1,2,0:T(8,128)} %param.17) | copy-start | bytes 786436
  4.7 134.4 %copy-start = (f32[2,512,64]{2,1,0:T(8,128)S(1)}, f32[2,512,64]{2,1,0:T(8,128)}, u32[]{:S(2)}) copy-start(f32[2,512,64]{2,1,0:T(8,128)} %copy.25.down_hbm) | copy-start | bytes 786436

commit v2 on v1

--- a/solution.py
+++ b/solution.py
@@ -11,6 +11,7 @@
 LANGS = 16
 RANK = 64
 ROWS_OWN = 512
+GROUP = 4
 FEATURES = 512
 KEYS = 1024
 
@@ -26,7 +27,7 @@
 LAST = (((1,), (1,)), ((), ()))
 FIRST = (((0,), (0,)), ((), ()))
 CUT = 144
-CHIPS = [(1, 0), (3, 0), (2, 0), (0, 1), (1, 1), (3, 1), (2, 1)]
+RING = (1, 3, 2)
 PLANE = [(dy, dz) for dz in range(4) for dy in range(4) if (dy, dz) != (0, 0)]
 DATA = [(dx, dl) for dl in range(2) for dx in range(4) if (dx, dl) != (0, 0)]
 
@@ -38,6 +39,10 @@
     second_hat = new_second / (1.0 - beta_second**STEP)
     new_param = param - learn_rate * first_hat / (jnp.sqrt(second_hat) + adam_epsilon)
     return (new_param, new_first, new_second)
+
+
+def turn(a):
+    return jnp.swapaxes(a, 1, 2)
 
 
 def block_layout(counts, slot_language, first_block):
@@ -57,8 +62,8 @@
 def kernel(
     slot_ref, left_ref, acts_hbm, grad_hbm, base_hbm, down_hbm, up_hbm,
     out_hbm, down_out, up_out,
-    G, ACT, BASE, WT, DOWN, UPOWN, UP, UMINE, USIB, DT, BK, LW, LOWN, LSIB, LGOT, LSUM, LARR,
-    DG, DSEND, DARR, DZ, DZARR, UG, USEND, UARR, EXP, OB, send_sems, recv_sems, local_sems, out_sems,
+    G, ACT, BASE, WT, DOWN, UPOWN, UP, UMINE, USIB, DT, BK, LW, LOWN, LSIB, LGOT, LSUM, LARR, LZ, LZARR,
+    DG, DSEND, DARR, DZ, DZARR, UG, UOTHER, UHALF, USEND, UARR, EXP, OB, send_sems, recv_sems, local_sems, out_sems,
 ):
     dp, f = lax.axis_index("dp"), lax.axis_index("fsdp")
     x, zl = lax.rem(dp, 4), dp // 4
@@ -134,7 +139,9 @@
     rows("c4", 2, 0, 0, n, **sibling)
     rows("c5", 3, 1, 0, n, **sibling)
     rows("c6", 1, 1, 0, n, **sibling)
-    rows("c7", 2, 1, 0, n, **sibling)
+    rows("c7m", 2, 1, top, low_end, **sibling)
+    rows("c70", 2, 1, 0, top, **sibling)
+    rows("c71", 2, 1, low_end, n, **sibling)
     message("u0", lambda: UMINE, lambda: USIB, lambda: at(dc=1))
     for k, (dy, dz) in enumerate(PLANE):
         same(
@@ -154,15 +161,23 @@
                 lambda l=l: DT.at[pl.ds(((zl + l) % 2 * 4 + x) * 2, 2)],
                 lambda dx=dx: at(dx=dx),
             )
-    for k, (dy, dh) in enumerate(CHIPS):
-        to = lambda dy=dy, dh=dh: at(dy=dy, dz=2 * dh)
-        same(f"b_{k}", lambda: BK.at[chip, c], to)
-        message(
-            f"l1_{k}", lambda dy=dy, dh=dh: LSUM.at[chip_of(dy, dh)], lambda k=k: LARR.at[k], to
-        )
-        same(f"l2_{k}", lambda: LW.at[chip, c], to)
+    other = chip_of(0, 1)
+    for k, dy in enumerate(RING):
+        to = lambda dy=dy: at(dy=dy)
+        for l in (0, 1):
+            message(
+                f"ly_{k}_{l}",
+                lambda dy=dy, l=l: LSUM.at[chip_of(dy, l)],
+                lambda k=k, l=l: LARR.at[k, l],
+                to,
+            )
+            same(f"b_{k}_{l}", lambda l=l: BK.at[chip_of(0, l), c], to)
+            same(f"w_{k}_{l}", lambda l=l: LW.at[chip_of(0, l)], to)
+    message("lz", lambda: LZ, lambda: LZARR, lambda: at(dz=2))
+    same("bz", lambda: BK.at[chip, c], lambda: at(dz=2))
+    same("wz", lambda: LW.at[chip], lambda: at(dz=2))
+    message("ux", lambda: UOTHER, lambda: UHALF, lambda: at(dc=1))
     same("b_c", lambda: BK.at[:, c], lambda: at(dc=1))
-    same("l2_c", lambda: LW.at[:, c], lambda: at(dc=1))
     message("l0", lambda: LSIB, lambda: LGOT, lambda: at(dc=1))
     for k, dx in enumerate((1, 3, 2)):
         for l in (0, 1):
@@ -204,35 +219,30 @@
         jnp.concatenate([own_up, none], axis=1) * first_core
         + jnp.concatenate([none, own_up], axis=1) * (1.0 - first_core)
     ).astype(BF16)
+    loads[2].wait()
+    for s in range(2):
+        DT[dp * 2 + s] = DOWN[s].astype(BF16)
+    pl.semaphore_wait(barrier, len(peers))
+    start("u0", "d0")
     loads[1].wait()
     for j in range(4):
         inside = lax.broadcasted_iota(jnp.int32, (BLK, KEYS), 0) < left_ref[f * 4 + j]
         part = G[f, pl.ds(j * BLK, BLK)].astype(F32)
         G[f, pl.ds(j * BLK, BLK)] = jnp.where(inside, part, 0.0).astype(BF16)
-    pl.semaphore_wait(barrier, len(peers))
-
-    start("u0")
-    loads[2].wait()
-    for s in range(2):
-        DT[dp * 2 + s] = DOWN[s].T.astype(BF16)
-    start("d0")
-    start("yp0", "ym1", "zA0", "zA1", "yp1", "ym0", "zB", "c0")
     got("u0")
     mine, theirs = UMINE[pl.ds(c * RANK, RANK)], USIB[pl.ds(c * RANK, RANK)]
     UP[dp, c, :, pl.ds(pl.multiple_of(chip * 128, 128), 128)] = (
         mine.astype(F32) + theirs.astype(F32)
     ).astype(BF16)
     start(*[f"u1_{k}" for k in range(len(PLANE))])
+    start("yp0", "ym1", "zA0", "zA1")
     got("d0")
     start(*[f"d1_{dx}_{l}" for dx in (1, 3, 2) for l in (0, 1)])
+    start("yp1", "ym0", "zB", "c0")
+    loads[3].wait()
+    WT[...] = BASE[...].T
     got(*[f"u1_{k}" for k in range(len(PLANE))])
     start(*[f"u2_{dx}_{l}" for dx in (1, 3, 2) for l in (0, 1)])
-    loads[3].wait()
-    WT[...] = BASE[...].T
-    got("zA0")
-    start("ap0", "am0")
-    got("zA1")
-    start("ap1", "am1")
     got(*[f"d1_{dx}_{l}" for dx in (1, 3, 2) for l in (0, 1)])
     loads[4].wait()
 
@@ -246,23 +256,13 @@
         return jnp.concatenate(parts, axis=1)
 
     def low_step(q, _):
-        @pl.when(q == 2)
-        def _():
-            got("yp0")
-            start("fp")
-            got("ym1")
-            start("fm")
-
         LSIB[q] = partial_low(q * 2 + 1 - c).astype(BF16)
         LOWN[q] = partial_low(q * 2 + c)
         return 0
 
     lax.fori_loop(0, 8, low_step, 0)
     start("l0")
-    got("yp1")
-    start("zBm", "c1")
-    got("ym0")
-    start("zBp", "c2")
+    got("zA0", "yp0", "ym1")
     got("l0")
 
     def sum_step(q, _):
@@ -272,68 +272,79 @@
         return 0
 
     lax.fori_loop(0, 8, sum_step, 0)
-    start(*[f"l1_{k}" for k in range(7)])
+    both = [f"{k}_{l}" for k in range(3) for l in (0, 1)]
+    start(*["ly_" + k for k in both])
 
     got(*[f"u2_{dx}_{l}" for dx in (1, 3, 2) for l in (0, 1)])
     start("u3")
-    got("u3")
+    got("zA1", "u3")
     for j in range(4):
         s = slot_ref[f * 4 + j]
         BK[chip, c, :, pl.ds(j * BLK, BLK)] = lax.dot_general(
             UP[s // 2, s % 2], G[f, pl.ds(j * BLK, BLK)], LAST, preferred_element_type=F32
         ).astype(BF16)
-    start(*[f"b_{k}" for k in range(7)])
+    start("bz", *[f"b_{k}_0" for k in range(3)])
+    got("yp1")
+    start("c1")
+    got("ym0")
+    start("c2")
+    got("bz")
+    start(*[f"b_{k}_1" for k in range(3)])
+    start("fp", "fm")
+    got(*["ly_" + k for k in both])
+    total = LOWN[other]
+    for k in range(3):
+        total += LARR[k, 1].astype(F32)
+    LZ[...] = total.astype(BF16)
+    start("lz", "zBm")
     got("zB")
     start("c3")
-    got(*[f"l1_{k}" for k in range(7)])
     total = LOWN[chip]
-    for k in range(7):
-        total += LARR[k].astype(F32)
-    LW[chip, c] = total.astype(BF16)
-    start(*[f"l2_{k}" for k in range(7)])
-    got(*[f"b_{k}" for k in range(7)])
-    start("b_c")
-    got("ap0")
-    start("fap")
-    got("am1")
-    start("fam")
+    for k in range(3):
+        total += LARR[k, 0].astype(F32)
+    got("lz")
+    LW[chip] = (total + LZARR[...].astype(F32)).astype(BF16)
+    start("wz", *[f"w_{k}_0" for k in range(3)])
+    start("zBp")
+    got(*["b_" + k for k in both])
+    start("b_c", "ap0", "am1")
     got("b_c")
 
-    def spread(source, fb):
+    def spread(read, fb, at_column):
         for j in range(4):
             slot = slot_ref[fb * 4 + j]
-            part = source[fb // 2, fb % 2, :, pl.ds(j * BLK, BLK)].astype(F32)
+            part = read(pl.ds(j * BLK, BLK)).astype(F32)
             for s in range(LANGS):
                 weight = jnp.where(slot == s, 1.0, 0.0).astype(F32)
-                EXP[pl.ds(s * RANK, RANK), pl.ds(j * BLK, BLK)] = (part * weight).astype(BF16)
-
-    def down_step(fb, _):
-        @pl.when(fb == 6)
-        def _():
-            got("fp", "fm")
-            start("zB2", "c4")
-
-        @pl.when(fb == 10)
-        def _():
-            got(*[f"l2_{k}" for k in range(7)])
-            start("l2_c")
-
-        spread(BK, fb)
-        part = jnp.dot(
-            EXP[...], ACT[pl.ds(fb * ROWS_OWN, ROWS_OWN)], preferred_element_type=F32
-        )
-
-        @pl.when(fb == 0)
+                EXP[pl.ds(s * RANK, RANK), pl.ds(at_column + j * BLK, BLK)] = (
+                    part * weight
+                ).astype(BF16)
+
+    span = GROUP * ROWS_OWN
+
+    def down_step(g, _):
+        @pl.when(g == 16 // GROUP - 1)
+        def _():
+            got("wz")
+            start(*[f"w_{k}_1" for k in range(3)])
+            start("ap1", "am0")
+
+        for i in range(GROUP):
+            fb = g * GROUP + i
+            spread(lambda cols: BK[fb // 2, fb % 2, :, cols], fb, i * ROWS_OWN)
+        part = jnp.dot(EXP[...], ACT[pl.ds(g * span, span)], preferred_element_type=F32)
+
+        @pl.when(g == 0)
         def _():
             DG[...] = part
 
-        @pl.when(fb > 0)
+        @pl.when(g > 0)
         def _():
             DG[...] += part
 
         return 0
 
-    lax.fori_loop(0, 16, down_step, 0)
+    lax.fori_loop(0, 16 // GROUP, down_step, 0)
 
     def scale_step(s, _):
         total = adapter_scale * DG[pl.ds(s * RANK, RANK)]
@@ -343,7 +354,9 @@
 
     lax.fori_loop(0, LANGS, scale_step, 0)
     start(*[f"r0_{k}_{l}" for k in range(3) for l in (0, 1)])
-    got("l2_c")
+    got(*[f"w_{k}_0" for k in range(3)])
+    got("fp", "fm")
+    start("zB2", "c4")
 
     order = [(0, 0), (3, 0), (1, 0), (0, 1), (2, 0), (3, 1), (1, 1), (2, 1)]
 
@@ -371,30 +384,40 @@
         def _():
             got("c0")
 
+        @pl.when(t == 2)
+        def _():
+            got("ap0")
+            start("fap")
+            got("am1")
+            start("fam")
+
         @pl.when(t == 3)
         def _():
             got("c1")
 
-        @pl.when(t == 4)
-        def _():
-            got("ap1", "zBm")
-            start("c5")
-
         @pl.when(t == 5)
         def _():
-            got("c2", "am0", "zBp")
-            start("c6")
+            got("c2")
+
+        @pl.when(t == 6)
+        def _():
+            got(*[f"w_{k}_1" for k in range(3)])
 
         @pl.when(t == 7)
         def _():
             got("c3")
+
+        @pl.when(t == 9)
+        def _():
+            got("c4")
             got(*[f"r0_{k}_{l}" for k in range(3) for l in (0, 1)])
             DZ[...] = down_sum(1 - zl).astype(BF16)
             start("r1")
 
-        @pl.when(t == 9)
-        def _():
-            got("c4")
+        @pl.when(t == 10)
+        def _():
+            got("zBm", "ap1")
+            start("c5")
 
         @pl.when(t == 11)
         def _():
@@ -402,33 +425,51 @@
 
         @pl.when(t == 12)
         def _():
-            got("fap", "fam", "zB2")
-            start("c7")
+            got("zBp", "am0")
+            start("c6")
 
         @pl.when(t == 13)
         def _():
             got("c6")
 
+        @pl.when(t == 14)
+        def _():
+            got("r1")
+            total = down_sum(zl) + DZARR[...].astype(F32)
+            down_out[0] = total[:RANK]
+            down_out[1] = total[RANK:]
+            got("zB2")
+            start("c7m")
+            got("fap")
+            start("c70")
+            got("fam")
+            start("c71")
+
         @pl.when(t == 15)
         def _():
-            got("c7")
-
-        spread(LW, fb)
-        part = jnp.dot(
-            EXP[...],
-            G[fb, :, pl.ds(pl.multiple_of(chip * 128, 128), 128)],
-            preferred_element_type=F32,
-        )
-
-        @pl.when(t == 0)
-        def _():
-            UG[...] = part
-
-        @pl.when(t > 0)
-        def _():
-            UG[...] += part
-
-        @pl.when(t == 15)
+            got("ux")
+            USEND[...] += UHALF[...]
+            start(*[f"v_{k}" for k in range(7)])
+            got("c7m", "c70", "c71")
+
+        @pl.when(core == 0)
+        def _():
+            spread(lambda cols: LW[fb // 2, :, cols], fb, 0)
+            part = jnp.dot(
+                EXP[:, :ROWS_OWN],
+                G[fb, :, pl.ds(pl.multiple_of(chip * 128, 128), 128)],
+                preferred_element_type=F32,
+            )
+
+            @pl.when(t == 0)
+            def _():
+                UG[...] = part
+
+            @pl.when(t > 0)
+            def _():
+                UG[...] += part
+
+        @pl.when(t == 14)
         def _():
             lane = lax.broadcasted_iota(jnp.int32, (RANK, 128), 1)
             for d in range(8):
@@ -437,7 +478,8 @@
                 left = jnp.where(lane < RANK, even, pltpu.roll(odd, RANK, 1))
                 right = jnp.where(lane < RANK, pltpu.roll(even, RANK, 1), odd)
                 USEND[d] = left * first_core + right * (1.0 - first_core)
-            start(*[f"v_{k}" for k in range(7)])
+                UOTHER[d] = right * first_core + left * (1.0 - first_core)
+            start("ux")
 
         slot = t % 2
 
@@ -460,10 +502,6 @@
         return 0
 
     lax.fori_loop(0, 16, main_step, 0)
-    got("r1")
-    total = down_sum(zl) + DZARR[...].astype(F32)
-    down_out[0] = total[:RANK].T
-    down_out[1] = total[RANK:].T
     got(*[f"v_{k}" for k in range(7)])
     total = USEND[dp]
     for k in range(7):
@@ -497,7 +535,7 @@
         kernel,
         out_shape=(
             jax.ShapeDtypeStruct(activations.shape, BF16),
-            jax.ShapeDtypeStruct((2, FEATURES, RANK), F32),
+            jax.ShapeDtypeStruct((2, RANK, FEATURES), F32),
             jax.ShapeDtypeStruct((RANK, 128), F32),
         ),
         in_specs=[smem, smem] + [anywhere] * 5,
@@ -507,19 +545,21 @@
             pltpu.VMEM((16 * ROWS_OWN, FEATURES), BF16),
             pltpu.VMEM((FEATURES, KEYS), BF16),
             pltpu.VMEM((KEYS, FEATURES), BF16),
-            pltpu.VMEM((2, FEATURES, RANK), F32),
+            pltpu.VMEM((2, RANK, FEATURES), F32),
             pltpu.VMEM((2, RANK, RANK), F32),
             pltpu.VMEM((8, 2, RANK, KEYS), BF16),
             pltpu.VMEM((2 * RANK, 128), BF16),
             pltpu.VMEM((2 * RANK, 128), BF16),
             pltpu.VMEM((LANGS, RANK, FEATURES), BF16),
             pltpu.VMEM((8, 2, RANK, ROWS_OWN), BF16),
-            pltpu.VMEM((8, 2, RANK, ROWS_OWN), BF16),
+            pltpu.VMEM((8, RANK, ROWS_OWN), BF16),
             pltpu.VMEM((8, RANK, ROWS_OWN), F32),
             pltpu.VMEM((8, RANK, ROWS_OWN), BF16),
             pltpu.VMEM((8, RANK, ROWS_OWN), BF16),
             pltpu.VMEM((8, RANK, ROWS_OWN), BF16),
-            pltpu.VMEM((7, RANK, ROWS_OWN), BF16),
+            pltpu.VMEM((3, 2, RANK, ROWS_OWN), BF16),
+            pltpu.VMEM((RANK, ROWS_OWN), BF16),
+            pltpu.VMEM((RANK, ROWS_OWN), BF16),
             pltpu.VMEM((LANGS * RANK, FEATURES), F32),
             pltpu.VMEM((LANGS, RANK, FEATURES), BF16),
             pltpu.VMEM((3, 2, 2, RANK, FEATURES), BF16),
@@ -527,8 +567,10 @@
             pltpu.VMEM((2 * RANK, FEATURES), BF16),
             pltpu.VMEM((LANGS * RANK, 128), F32),
             pltpu.VMEM((8, RANK, 128), F32),
+            pltpu.VMEM((8, RANK, 128), F32),
+            pltpu.VMEM((8, RANK, 128), F32),
             pltpu.VMEM((7, RANK, 128), F32),
-            pltpu.VMEM((LANGS * RANK, ROWS_OWN), BF16),
+            pltpu.VMEM((LANGS * RANK, GROUP * ROWS_OWN), BF16),
             pltpu.VMEM((2, ROWS_OWN, FEATURES), BF16),
             pltpu.SemaphoreType.DMA((n_messages,)),
             pltpu.SemaphoreType.DMA((n_messages,)),
@@ -541,10 +583,10 @@
         cost_estimate=pl.CostEstimate(
             flops=2 * 8192 * 512 * 1024 * 3, bytes_accessed=40 * 2**20, transcendentals=0
         ),
-    )(slots, left, activations, grad_out, base_weight, down_param, up_param)
+    )(slots, left, activations, grad_out, base_weight, turn(down_param), up_param)
     up_gradient = jnp.stack([up_own[:, :RANK], up_own[:, RANK:]])
-    new_down, new_down_first, new_down_second = adam_update(
-        down_param, down_first, down_second, down_own
+    new_down, new_down_first, new_down_second = map(
+        turn, adam_update(turn(down_param), turn(down_first), turn(down_second), down_own)
     )
     new_up, new_up_first, new_up_second = adam_update(up_param, up_first, up_second, up_gradient)
     return (

time: 151 us -> 112 us (0.74)
  Pallas kernels: 132 us -> 98 us
  local copies, waits for them, and re-layouts: 13.2 us -> 8.25 us
    pallas_call x1, Pallas kernels: 132 us -> 98 us  [on_device(): pl.pallas_call(kernel, out_shape=(jax.ShapeDtypeStruct(activations.shape,...]
    unnamed x19 -> x13, local copies, waits for them, and re-layouts: 12.3 us -> 7.34 us
    transpose x0 -> x1, other arithmetic: none -> 1.99 us  [turn(): return jnp.swapaxes(a, 1, 2)]
where the time goes in v2:
time: 112 us
  Pallas kernels  98 us (88%)
  local copies, waits for them, and re-layouts  8.25 us (7%)
  other arithmetic  4.82 us (4%)
    pallas_call x1, Pallas kernels, on_device(): pl.pallas_call(kernel, out_shape=(jax.ShapeDtypeStruct(activations.shape,...  98 us
    unnamed x13, local copies, waits for them, and re-layouts  7.34 us

profile of v2, /device:TPU:1, one launch (start us, length us, event | category | flops | bytes accessed | tf_op | source)
XLA Modules:
  0.0 111.8 jit_solution(2906517864800427428)
XLA Ops:
  0.6 0.7 and_select_fusion
  1.3 0.9 select_reduce_fusion.2
  2.2 0.6 fusion.7
  2.8 0.0 copy-start.3
  2.8 0.0 copy-start.4
  2.8 0.0 copy-start.5
  2.8 0.0 copy-start
  2.8 0.0 copy-start.1
  2.8 0.0 copy-start.2
  2.8 98.0 %shard_map.162 = (bf16[8192,512]{1,0:T(8,128)(2,1)}, f32[2,64,512]{2,1,0:T(8,128)}, f32[64,128]{1,0:T(8,128)}) custom-call(s32[64]{0:T(128)} %get-tuple-element.14.slot_ref, s32[64]{0:T(128)} %get-tuple-element.13.left_ref, bf16[8192,512]{1,0:T(8,128)(2,1)} %acts_hbm.1, bf16[512,1024]{1,0:T(8,128)(2,1)} %grad_hbm.1, bf16[512,1024]{1,0:T(8,128)(2,1)} %base_hbm.1, ...), custom_call_target="tpu_custom_call" | custom-call | flops 25769803776 | bytes 41943040 | tf_op jit(solution)/shard_map/pallas_call | solution.py:534
  100.9 0.9 slice_bitcast_fusion.1
  101.8 0.0 copy-done.3
  101.8 0.0 copy-done.4
  101.8 0.0 copy-done.5
  101.8 0.7 divide_subtract_fusion
  102.5 0.0 copy-done
  102.5 0.0 copy-done.1
  102.5 0.0 copy-done.2
  102.5 2.0 %fusion.2 = (f32[2,512,64]{1,2,0:T(8,128)}, f32[2,512,64]{1,2,0:T(8,128)}, f32[2,512,64]{1,2,0:T(8,128)}) fusion(f32[2,64,512]{2,1,0:T(8,128)} %get-tuple-element.11, f32[2,512,64]{1,2,0:T(8,128)S(1)} %copy-done.1, f32[2,512,64]{1,2,0:T(8,128)S(1)} %copy-done.2, f32[2,512,64]{1,2,0:T(8,128)S(1)} %copy-done), kind=kLoop, calls=%fused_computation.6 | loop fusion | flops 786432 | bytes 1835008 | tf_op jit(solution)/shard_map/transpose | solution.py:45
  104.5 7.3 %copy.19 = bf16[8192,512]{1,0:T(8,128)(2,1)} copy(bf16[8192,512]{1,0:T(8,128)(2,1)} %get-tuple-element.32) | data formatting | bytes 16777216
  (1 shorter events, 0.0 us)
Async XLA Ops:
  2.8 99.0 %copy-start.3 = (f32[2,64,64]{2,1,0:T(8,128)S(1)}, f32[2,64,64]{2,1,0:T(8,128)}, u32[]{:S(2)}) copy-start(f32[2,64,64]{2,1,0:T(8,128)} %up_hbm.1) | copy-start | bytes 98308
  2.8 99.0 %copy-start.4 = (f32[2,64,64]{2,1,0:T(8,128)S(1)}, f32[2,64,64]{2,1,0:T(8,128)}, u32[]{:S(2)}) copy-start(f32[2,64,64]{2,1,0:T(8,128)} %param.18) | copy-start | bytes 98308
  2.8 99.0 %copy-start.5 = (f32[2,64,64]{2,1,0:T(8,128)S(1)}, f32[2,64,64]{2,1,0:T(8,128)}, u32[]{:S(2)}) copy-start(f32[2,64,64]{2,1,0:T(8,128)} %param.19) | copy-start | bytes 98308
  2.8 99.7 %copy-start = (f32[2,512,64]{1,2,0:T(8,128)S(1)}, f32[2,512,64]{1,2,0:T(8,128)}, u32[]{:S(2)}) copy-start(f32[2,512,64]{1,2,0:T(8,128)} %param.14) | copy-start | bytes 786436
  2.8 99.7 %copy-start.1 = (f32[2,512,64]{1,2,0:T(8,128)S(1)}, f32[2,512,64]{1,2,0:T(8,128)}, u32[]{:S(2)}) copy-start(f32[2,512,64]{1,2,0:T(8,128)} %param.17) | copy-start | bytes 786436
  2.8 99.7 %copy-start.2 = (f32[2,512,64]{1,2,0:T(8,128)S(1)}, f32[2,512,64]{1,2,0:T(8,128)}, u32[]{:S(2)}) copy-start(f32[2,512,64]{1,2,0:T(8,128)} %param.16) | copy-start | bytes 786436

commit v3 on v2

--- a/solution.py
+++ b/solution.py
@@ -28,7 +28,6 @@
 FIRST = (((0,), (0,)), ((), ()))
 CUT = 144
 RING = (1, 3, 2)
-PLANE = [(dy, dz) for dz in range(4) for dy in range(4) if (dy, dz) != (0, 0)]
 DATA = [(dx, dl) for dl in range(2) for dx in range(4) if (dx, dl) != (0, 0)]
 
 
@@ -63,7 +62,7 @@
     slot_ref, left_ref, acts_hbm, grad_hbm, base_hbm, down_hbm, up_hbm,
     out_hbm, down_out, up_out,
     G, ACT, BASE, WT, DOWN, UPOWN, UP, UMINE, USIB, DT, BK, LW, LOWN, LSIB, LGOT, LSUM, LARR, LZ, LZARR,
-    DG, DSEND, DARR, DZ, DZARR, UG, UOTHER, UHALF, USEND, UARR, EXP, OB, send_sems, recv_sems, local_sems, out_sems,
+    DG, DSEND, DARR, DZ, DZARR, UG, FAR, COLUMNS, UOTHER, UHALF, USEND, UARR, EXP, OB, send_sems, recv_sems, local_sems, out_sems,
 ):
     dp, f = lax.axis_index("dp"), lax.axis_index("fsdp")
     x, zl = lax.rem(dp, 4), dp // 4
@@ -143,12 +142,24 @@
     rows("c70", 2, 1, 0, top, **sibling)
     rows("c71", 2, 1, low_end, n, **sibling)
     message("u0", lambda: UMINE, lambda: USIB, lambda: at(dc=1))
-    for k, (dy, dz) in enumerate(PLANE):
+    for k, dy in enumerate(RING):
         same(
-            f"u1_{k}",
+            f"uy_{k}",
             lambda: UP.at[dp, c, :, pl.ds(pl.multiple_of(chip * 128, 128), 128)],
-            lambda dy=dy, dz=dz: at(dy=dy, dz=dz),
+            lambda dy=dy: at(dy=dy),
         )
+    for k, dz in enumerate((1, 3, 2)):
+        same(
+            f"uz_{k}",
+            lambda: UP.at[dp, c, :, pl.ds(pl.multiple_of(h * 512, 128), 512)],
+            lambda dz=dz: at(dz=dz),
+        )
+    message(
+        "q",
+        lambda: G.at[f, :, pl.ds(pl.multiple_of(chip_of(2, 1) * 128, 128), 128)],
+        lambda: FAR,
+        lambda: at(dy=2, dz=2),
+    )
     for dx in (1, 3, 2):
         for l in (0, 1):
             same(f"u2_{dx}_{l}", lambda l=l: UP.at[l * 4 + x, c], lambda dx=dx: at(dx=dx))
@@ -206,7 +217,7 @@
     for load in loads:
         load.start()
     barrier = pltpu.get_barrier_semaphore()
-    peers = [at(dy=dy, dz=dz) for dy, dz in PLANE] + [at(dc=1)]
+    peers = [at(dy=d) for d in RING] + [at(dz=d) for d in (1, 2, 3)] + [at(dc=1), at(dy=2, dz=2)]
     peers += [at(dx=dx) for dx in (1, 2, 3)] + [flip(dx) for dx in (1, 2, 3)]
     for peer in peers:
         pl.semaphore_signal(barrier, inc=1, device_id=peer, device_id_type=MESH)
@@ -234,15 +245,17 @@
     UP[dp, c, :, pl.ds(pl.multiple_of(chip * 128, 128), 128)] = (
         mine.astype(F32) + theirs.astype(F32)
     ).astype(BF16)
-    start(*[f"u1_{k}" for k in range(len(PLANE))])
-    start("yp0", "ym1", "zA0", "zA1")
+    start(*[f"uy_{k}" for k in range(3)])
     got("d0")
     start(*[f"d1_{dx}_{l}" for dx in (1, 3, 2) for l in (0, 1)])
-    start("yp1", "ym0", "zB", "c0")
+    got(*[f"uy_{k}" for k in range(3)])
+    start(*[f"uz_{k}" for k in range(3)])
+    start("yp0", "ym1", "yp1", "ym0", "c0")
+    got(*[f"uz_{k}" for k in range(3)])
+    start("zA0", "zA1", "zB")
+    start(*[f"u2_{dx}_{l}" for dx in (1, 3, 2) for l in (0, 1)])
     loads[3].wait()
     WT[...] = BASE[...].T
-    got(*[f"u1_{k}" for k in range(len(PLANE))])
-    start(*[f"u2_{dx}_{l}" for dx in (1, 3, 2) for l in (0, 1)])
     got(*[f"d1_{dx}_{l}" for dx in (1, 3, 2) for l in (0, 1)])
     loads[4].wait()
 
@@ -327,7 +340,7 @@
         def _():
             got("wz")
             start(*[f"w_{k}_1" for k in range(3)])
-            start("ap1", "am0")
+            start("q", "ap1", "am0")
 
         for i in range(GROUP):
             fb = g * GROUP + i
@@ -421,45 +434,44 @@
 
         @pl.when(t == 11)
         def _():
-            got("c5")
-
-        @pl.when(t == 12)
-        def _():
             got("zBp", "am0")
             start("c6")
+            got("c5")
 
         @pl.when(t == 13)
         def _():
-            got("c6")
+            got("q")
+            COLUMNS[...] = FAR[...]
 
         @pl.when(t == 14)
         def _():
-            got("r1")
-            total = down_sum(zl) + DZARR[...].astype(F32)
-            down_out[0] = total[:RANK]
-            down_out[1] = total[RANK:]
             got("zB2")
             start("c7m")
             got("fap")
             start("c70")
             got("fam")
             start("c71")
-
-        @pl.when(t == 15)
-        def _():
             got("ux")
             USEND[...] += UHALF[...]
             start(*[f"v_{k}" for k in range(7)])
+
+        @pl.when(t == 15)
+        def _():
+            got("r1")
+            total = down_sum(zl) + DZARR[...].astype(F32)
+            down_out[0] = total[:RANK]
+            down_out[1] = total[RANK:]
             got("c7m", "c70", "c71")
 
-        @pl.when(core == 0)
-        def _():
-            spread(lambda cols: LW[fb // 2, :, cols], fb, 0)
-            part = jnp.dot(
-                EXP[:, :ROWS_OWN],
-                G[fb, :, pl.ds(pl.multiple_of(chip * 128, 128), 128)],
-                preferred_element_type=F32,
-            )
+        @pl.when((core == 0) & (t < 14))
+        def _():
+            COLUMNS[...] = G[fb, :, pl.ds(pl.multiple_of(chip * 128, 128), 128)]
+
+        @pl.when(((core == 0) & (t < 14)) | (t == 13))
+        def _():
+            source = jnp.where(t == 13, chip_of(2, 1), fb // 2)
+            spread(lambda cols: LW[source, :, cols], source * 2 + c, 0)
+            part = jnp.dot(EXP[:, :ROWS_OWN], COLUMNS[...], preferred_element_type=F32)
 
             @pl.when(t == 0)
             def _():
@@ -469,7 +481,7 @@
             def _():
                 UG[...] += part
 
-        @pl.when(t == 14)
+        @pl.when(t == 13)
         def _():
             lane = lax.broadcasted_iota(jnp.int32, (RANK, 128), 1)
             for d in range(8):
@@ -480,6 +492,7 @@
                 USEND[d] = left * first_core + right * (1.0 - first_core)
                 UOTHER[d] = right * first_core + left * (1.0 - first_core)
             start("ux")
+            got("c6")
 
         slot = t % 2
 
@@ -511,6 +524,49 @@
     write(f, 1).wait()
     for name in makers:
         makers[name]().wait_send()
+
+
+def second_kernel(first_hbm, *refs):
+    ins, out_hbm, outs = refs[:8], refs[8], refs[9:15]
+    PIECES, scratch = refs[15], refs[16:30]
+    in_sems, piece_in, piece_out, out_sems = refs[30:]
+    loads = [
+        pltpu.make_async_copy(ins[k], scratch[k], in_sems.at[k]) for k in range(8)
+    ]
+    pieces = [pl.ds(k * ROWS_OWN, ROWS_OWN) for k in range(16)]
+    reads = [
+        pltpu.make_async_copy(first_hbm.at[rows], PIECES.at[k], piece_in.at[k])
+        for k, rows in enumerate(pieces)
+    ]
+    writes = [
+        pltpu.make_async_copy(PIECES.at[k], out_hbm.at[rows], piece_out.at[k])
+        for k, rows in enumerate(pieces)
+    ]
+    for copy in (*reads[:4], *loads, *reads[4:]):
+        copy.start()
+    for k in range(4):
+        reads[k].wait()
+        writes[k].start()
+    for copy in loads:
+        copy.wait()
+    down_grad, up_grad, down, down_first, down_second, up, up_first, up_second = scratch[:8]
+    results = scratch[8:]
+    for ref, value in zip(
+        results[:3], adam_update(down[...], down_first[...], down_second[...], down_grad[...])
+    ):
+        ref[...] = value
+    both = up_grad[...]
+    for s, gradient in enumerate((both[:, :RANK], pltpu.roll(both, RANK, 1)[:, :RANK])):
+        for ref, value in zip(results[3:], adam_update(up[s], up_first[s], up_second[s], gradient)):
+            ref[s] = value
+    stores = [pltpu.make_async_copy(results[k], outs[k], out_sems.at[k]) for k in range(6)]
+    for copy in stores:
+        copy.start()
+    for k in range(4, 16):
+        reads[k].wait()
+        writes[k].start()
+    for copy in (*writes, *stores):
+        copy.wait()
 
 
 def on_device(
@@ -531,7 +587,7 @@
     anywhere = pl.BlockSpec(memory_space=pl.ANY)
     vmem = pl.BlockSpec(memory_space=pltpu.VMEM)
     n_messages = 120
-    input_gradient, down_own, up_own = pl.pallas_call(
+    first_out, down_own, up_own = pl.pallas_call(
         kernel,
         out_shape=(
             jax.ShapeDtypeStruct(activations.shape, BF16),
@@ -566,6 +622,8 @@
             pltpu.VMEM((2 * RANK, FEATURES), BF16),
             pltpu.VMEM((2 * RANK, FEATURES), BF16),
             pltpu.VMEM((LANGS * RANK, 128), F32),
+            pltpu.VMEM((ROWS_OWN, 128), BF16),
+            pltpu.VMEM((ROWS_OWN, 128), BF16),
             pltpu.VMEM((8, RANK, 128), F32),
             pltpu.VMEM((8, RANK, 128), F32),
             pltpu.VMEM((8, RANK, 128), F32),
@@ -584,11 +642,30 @@
             flops=2 * 8192 * 512 * 1024 * 3, bytes_accessed=40 * 2**20, transcendentals=0
         ),
     )(slots, left, activations, grad_out, base_weight, turn(down_param), up_param)
-    up_gradient = jnp.stack([up_own[:, :RANK], up_own[:, RANK:]])
+    down_shape, up_shape = (2, RANK, FEATURES), (2, RANK, RANK)
+    shapes = [down_shape] * 3 + [up_shape] * 3
+    input_gradient, new_down, new_down_first, new_down_second, new_up, new_up_first, new_up_second = (
+        pl.pallas_call(
+            second_kernel,
+            out_shape=[jax.ShapeDtypeStruct(activations.shape, BF16)]
+            + [jax.ShapeDtypeStruct(shape, F32) for shape in shapes],
+            in_specs=[anywhere] * 9,
+            out_specs=[anywhere] * 7,
+            scratch_shapes=[pltpu.VMEM((16, ROWS_OWN, FEATURES), BF16)]
+            + [pltpu.VMEM(shape, F32) for shape in [down_shape, (RANK, 128)] + shapes + shapes]
+            + [pltpu.SemaphoreType.DMA((k,)) for k in (8, 16, 16, 6)],
+            compiler_params=pltpu.CompilerParams(vmem_limit_bytes=60 * 2**20),
+            cost_estimate=pl.CostEstimate(
+                flops=2**20, bytes_accessed=20 * 2**20, transcendentals=0
+            ),
+        )(
+            first_out, down_own, up_own,
+            turn(down_param), turn(down_first), turn(down_second), up_param, up_first, up_second,
+        )
+    )
     new_down, new_down_first, new_down_second = map(
-        turn, adam_update(turn(down_param), turn(down_first), turn(down_second), down_own)
+        turn, (new_down, new_down_first, new_down_second)
     )
-    new_up, new_up_first, new_up_second = adam_update(up_param, up_first, up_second, up_gradient)
     return (
         input_gradient,
         new_down,

time: 112 us -> 109 us (0.973)
  local copies, waits for them, and re-layouts: 8.25 us -> 0 us
  Pallas kernels: 98 us -> 106 us
  other arithmetic: 4.82 us -> 2.13 us
    pallas_call x0 -> x1, Pallas kernels: none -> 7.99 us  [on_device(): pl.pallas_call(second_kernel, out_shape=[jax.ShapeDtypeStruct(activations...]
    unnamed x13 -> x0, local copies, waits for them, and re-layouts: 7.34 us -> none
    transpose x1 -> x0, other arithmetic: 1.99 us -> none  [turn(): return jnp.swapaxes(a, 1, 2)]
where the time goes in v3:
time: 109 us
  Pallas kernels  106 us (97%)
  other arithmetic  2.13 us (2%)
    pallas_call x1, Pallas kernels, on_device(): pl.pallas_call(kernel, out_shape=(jax.ShapeDtypeStruct(activations.shape,...  98 us
    pallas_call x1, Pallas kernels, on_device(): pl.pallas_call(second_kernel, out_shape=[jax.ShapeDtypeStruct(activations...  7.99 us

profile of v3, /device:TPU:1, one launch (start us, length us, event | category | flops | bytes accessed | tf_op | source)
XLA Modules:
  0.0 108.8 jit_solution(7352495851614743558)
XLA Ops:
  0.6 0.7 and_select_fusion
  1.3 0.9 select_reduce_fusion.2
  2.2 0.6 fusion.3
  2.8 98.0 %shard_map.162 = (bf16[8192,512]{1,0:T(8,128)(2,1)}, f32[2,64,512]{2,1,0:T(8,128)}, f32[64,128]{1,0:T(8,128)}) custom-call(s32[64]{0:T(128)} %get-tuple-element.28.slot_ref, s32[64]{0:T(128)} %get-tuple-element.27.left_ref, bf16[8192,512]{1,0:T(8,128)(2,1)} %acts_hbm.1, bf16[512,1024]{1,0:T(8,128)(2,1)} %grad_hbm.1, bf16[512,1024]{1,0:T(8,128)(2,1)} %base_hbm.1, ...), custom_call_target="tpu_custom_call" | custom-call | flops 25769803776 | bytes 41943040 | tf_op jit(solution)/shard_map/pallas_call | solution.py:590
  100.8 8.0 %shard_map.163 = (bf16[8192,512]{1,0:T(8,128)(2,1)}, f32[2,64,512]{2,1,0:T(8,128)}, f32[2,64,512]{2,1,0:T(8,128)}, f32[2,64,512]{2,1,0:T(8,128)}, f32[2,64,64]{2...) custom-call(bf16[8192,512]{1,0:T(8,128)(2,1)} %get-tuple-element.17.first_hbm, ...), custom_call_target="tpu_custom_call" | custom-call | flops 1048576 | bytes 20971520 | tf_op jit(solution)/shard_map/pallas_call | solution.py:648
  (1 shorter events, 0.0 us)

commit v4 on v3

--- a/solution.py
+++ b/solution.py
@@ -26,7 +26,7 @@
 BF16 = jnp.bfloat16
 LAST = (((1,), (1,)), ((), ()))
 FIRST = (((0,), (0,)), ((), ()))
-CUT = 144
+CUT = 128
 RING = (1, 3, 2)
 DATA = [(dx, dl) for dl in range(2) for dx in range(4) if (dx, dl) != (0, 0)]
 
@@ -44,25 +44,12 @@
     return jnp.swapaxes(a, 1, 2)
 
 
-def block_layout(counts, slot_language, first_block):
-    ids = jnp.arange(LANGS, dtype=jnp.int32)
-    owner = slot_language[:, None]
-    count = jnp.sum(jnp.where(ids[None, :] == owner, counts[None, :], 0), axis=1)
-    start = jnp.sum(jnp.where(ids[None, :] < owner, (counts[None, :] + BLK - 1) // BLK, 0), axis=1)
-    behind = first_block + jnp.arange(BLOCKS_DP, dtype=jnp.int32)[:, None] - start[None, :]
-    left = count[None, :] - behind * BLK
-    hot = (behind >= 0) & (left > 0)
-    return (
-        jnp.sum(jnp.where(hot, ids[None, :], 0), axis=1),
-        jnp.sum(jnp.where(hot, left, 0), axis=1),
-    )
-
-
 def kernel(
-    slot_ref, left_ref, acts_hbm, grad_hbm, base_hbm, down_hbm, up_hbm,
+    count_ref, language_ref, acts_hbm, grad_hbm, base_hbm, down_hbm, up_hbm,
     out_hbm, down_out, up_out,
     G, ACT, BASE, WT, DOWN, UPOWN, UP, UMINE, USIB, DT, BK, LW, LOWN, LSIB, LGOT, LSUM, LARR, LZ, LZARR,
     DG, DSEND, DARR, DZ, DZARR, UG, FAR, COLUMNS, UOTHER, UHALF, USEND, UARR, EXP, OB, send_sems, recv_sems, local_sems, out_sems,
+    language_start, slot_start, slot_count, slot_ref,
 ):
     dp, f = lax.axis_index("dp"), lax.axis_index("fsdp")
     x, zl = lax.rem(dp, 4), dp // 4
@@ -160,16 +147,20 @@
         lambda: FAR,
         lambda: at(dy=2, dz=2),
     )
-    for dx in (1, 3, 2):
+    for dx in (1, 3):
         for l in (0, 1):
             same(f"u2_{dx}_{l}", lambda l=l: UP.at[l * 4 + x, c], lambda dx=dx: at(dx=dx))
+    same("u2_f1", lambda: UP.at[lax.rem(x + 3, 4), c], lambda: at(dx=1))
+    same("u2_f3", lambda: UP.at[4 + lax.rem(x + 1, 4), c], lambda: at(dx=3))
     same("u3", lambda: UP.at[:, c], lambda: at(dc=1))
     same("d0", lambda: DT.at[pl.ds(dp * 2, 2)], lambda: flip(0))
-    for dx in (1, 3, 2):
+    same("d1_f1", lambda: DT.at[pl.ds(lax.rem(x + 3, 4) * 2, 2)], lambda: at(dx=1))
+    same("d1_f3", lambda: DT.at[pl.ds((4 + lax.rem(x + 1, 4)) * 2, 2)], lambda: at(dx=3))
+    for dx in (1, 3):
         for l in (0, 1):
             same(
                 f"d1_{dx}_{l}",
-                lambda l=l: DT.at[pl.ds(((zl + l) % 2 * 4 + x) * 2, 2)],
+                lambda l=l: DT.at[pl.ds((l * 4 + x) * 2, 2)],
                 lambda dx=dx: at(dx=dx),
             )
     other = chip_of(0, 1)
@@ -222,6 +213,25 @@
     for peer in peers:
         pl.semaphore_signal(barrier, inc=1, device_id=peer, device_id_type=MESH)
 
+    running = jnp.int32(0)
+    for l in range(LANGS):
+        language_start[l] = running
+        running += (count_ref[l] + BLK - 1) // BLK
+    for s in range(LANGS):
+        slot_start[s] = language_start[language_ref[s]]
+        slot_count[s] = count_ref[language_ref[s]]
+
+    def layout(b):
+        slot, live = jnp.int32(0), jnp.int32(0)
+        for s in range(LANGS):
+            behind = dp * BLOCKS_DP + b - slot_start[s]
+            left = slot_count[s] - behind * BLK
+            hot = (behind >= 0) & (left > 0)
+            slot, live = jnp.where(hot, s, slot), jnp.where(hot, left, live)
+        return slot, live
+
+    live_rows = [layout(f * 4 + j)[1] for j in range(4)]
+
     loads[0].wait()
     own_up = UPOWN[...].reshape(2 * RANK, RANK)
     none = jnp.zeros_like(own_up)
@@ -237,7 +247,7 @@
     start("u0", "d0")
     loads[1].wait()
     for j in range(4):
-        inside = lax.broadcasted_iota(jnp.int32, (BLK, KEYS), 0) < left_ref[f * 4 + j]
+        inside = lax.broadcasted_iota(jnp.int32, (BLK, KEYS), 0) < live_rows[j]
         part = G[f, pl.ds(j * BLK, BLK)].astype(F32)
         G[f, pl.ds(j * BLK, BLK)] = jnp.where(inside, part, 0.0).astype(BF16)
     got("u0")
@@ -247,16 +257,31 @@
     ).astype(BF16)
     start(*[f"uy_{k}" for k in range(3)])
     got("d0")
-    start(*[f"d1_{dx}_{l}" for dx in (1, 3, 2) for l in (0, 1)])
+    start(*[f"d1_{dx}_{l}" for l in (0, 1) for dx in (1, 3)])
     got(*[f"uy_{k}" for k in range(3)])
     start(*[f"uz_{k}" for k in range(3)])
     start("yp0", "ym1", "yp1", "ym0", "c0")
     got(*[f"uz_{k}" for k in range(3)])
     start("zA0", "zA1", "zB")
-    start(*[f"u2_{dx}_{l}" for dx in (1, 3, 2) for l in (0, 1)])
+    start(*[f"u2_{dx}_{l}" for l in (0, 1) for dx in (1, 3)])
+
+    def slot_step(b, _):
+        slot_ref[b] = layout(b)[0]
+        return 0
+
+    lax.fori_loop(0, BLOCKS_DP, slot_step, 0)
     loads[3].wait()
     WT[...] = BASE[...].T
-    got(*[f"d1_{dx}_{l}" for dx in (1, 3, 2) for l in (0, 1)])
+    got("d1_1_0")
+    start("d1_f1")
+    got("d1_3_1")
+    start("d1_f3")
+    got("d1_1_1", "d1_3_0")
+    got("u2_1_0")
+    start("u2_f1")
+    got("u2_3_1")
+    start("u2_f3")
+    got("d1_f1", "d1_f3")
     loads[4].wait()
 
     def partial_low(fb):
@@ -275,6 +300,8 @@
 
     lax.fori_loop(0, 8, low_step, 0)
     start("l0")
+    got("u2_1_1", "u2_3_0", "u2_f1", "u2_f3")
+    start("u3")
     got("zA0", "yp0", "ym1")
     got("l0")
 
@@ -288,8 +315,6 @@
     both = [f"{k}_{l}" for k in range(3) for l in (0, 1)]
     start(*["ly_" + k for k in both])
 
-    got(*[f"u2_{dx}_{l}" for dx in (1, 3, 2) for l in (0, 1)])
-    start("u3")
     got("zA1", "u3")
     for j in range(4):
         s = slot_ref[f * 4 + j]
@@ -582,7 +607,6 @@
     counts,
     slot_language,
 ):
-    slots, left = block_layout(counts, slot_language, lax.axis_index("dp") * BLOCKS_DP)
     smem = pl.BlockSpec(memory_space=pltpu.SMEM)
     anywhere = pl.BlockSpec(memory_space=pl.ANY)
     vmem = pl.BlockSpec(memory_space=pltpu.VMEM)
@@ -634,6 +658,10 @@
             pltpu.SemaphoreType.DMA((n_messages,)),
             pltpu.SemaphoreType.DMA((5,)),
             pltpu.SemaphoreType.DMA((2,)),
+            pltpu.SMEM((LANGS,), jnp.int32),
+            pltpu.SMEM((LANGS,), jnp.int32),
+            pltpu.SMEM((LANGS,), jnp.int32),
+            pltpu.SMEM((BLOCKS_DP,), jnp.int32),
         ],
         compiler_params=pltpu.CompilerParams(
             collective_id=0, has_side_effects=True, vmem_limit_bytes=58 * 2**20
@@ -641,7 +669,7 @@
         cost_estimate=pl.CostEstimate(
             flops=2 * 8192 * 512 * 1024 * 3, bytes_accessed=40 * 2**20, transcendentals=0
         ),
-    )(slots, left, activations, grad_out, base_weight, turn(down_param), up_param)
+    )(counts, slot_language, activations, grad_out, base_weight, turn(down_param), up_param)
     down_shape, up_shape = (2, RANK, FEATURES), (2, RANK, RANK)
     shapes = [down_shape] * 3 + [up_shape] * 3
     input_gradient, new_down, new_down_first, new_down_second, new_up, new_up_first, new_up_second = (

time: 109 us -> 105 us (0.963)
  other arithmetic: 2.13 us -> 0 us
    reduce_sum x2 -> x0, other arithmetic: 1.46 us -> none  [the longest x1 0.85 us: block_layout(): jnp.sum(jnp.where(ids[None, :] < owner, (counts[None, :] + BLK - 1) // BL...]
    pallas_call x1, Pallas kernels: 98 us -> 96.7 us  [on_device(): pl.pallas_call(kernel, out_shape=(jax.ShapeDtypeStruct(activations.shape,...]
where the time goes in v4:
time: 105 us
  Pallas kernels  105 us (100%)
    pallas_call x1, Pallas kernels, on_device(): pl.pallas_call(kernel, out_shape=(jax.ShapeDtypeStruct(activations.shape,...  96.7 us
    pallas_call x1, Pallas kernels, on_device(): pl.pallas_call(second_kernel, out_shape=[jax.ShapeDtypeStruct(activations...  7.99 us

profile of v4, /device:TPU:1, one launch (start us, length us, event | category | flops | bytes accessed | tf_op | source)
XLA Modules:
  0.0 105.3 jit_solution(15560750783052285379)
XLA Ops:
  0.6 96.7 %shard_map.162 = (bf16[8192,512]{1,0:T(8,128)(2,1)}, f32[2,64,512]{2,1,0:T(8,128)}, f32[64,128]{1,0:T(8,128)}) custom-call(s32[16]{0:T(128)} %count_ref.1, s32[16]{0:T(128)} %language_ref.1, bf16[8192,512]{1,0:T(8,128)(2,1)} %acts_hbm.1, bf16[512,1024]{1,0:T(8,128)(2,1)} %grad_hbm.1, bf16[512,1024]{1,0:T(8,128)(2,1)} %base_hbm.1, f32[2,64,512]{2,1,0:T(8,128)} %bitcast.6, ...), custom_call_target="tpu_custom_call" | custom-call | flops 25769803776 | bytes 41943040 | tf_op jit(solution)/shard_map/pallas_call | solution.py:614
  97.3 8.0 %shard_map.163 = (bf16[8192,512]{1,0:T(8,128)(2,1)}, f32[2,64,512]{2,1,0:T(8,128)}, f32[2,64,512]{2,1,0:T(8,128)}, f32[2,64,512]{2,1,0:T(8,128)}, f32[2,64,64]{2...) custom-call(bf16[8192,512]{1,0:T(8,128)(2,1)} %get-tuple-element.17.first_hbm, ...), custom_call_target="tpu_custom_call" | custom-call | flops 1048576 | bytes 20971520 | tf_op jit(solution)/shard_map/pallas_call | solution.py:676

commit v5 on v4

--- a/solution.py
+++ b/solution.py
@@ -448,6 +448,9 @@
         @pl.when(t == 9)
         def _():
             got("c4")
+
+        @pl.when(t == 12)
+        def _():
             got(*[f"r0_{k}_{l}" for k in range(3) for l in (0, 1)])
             DZ[...] = down_sum(1 - zl).astype(BF16)
             start("r1")
@@ -567,9 +570,9 @@
         pltpu.make_async_copy(PIECES.at[k], out_hbm.at[rows], piece_out.at[k])
         for k, rows in enumerate(pieces)
     ]
-    for copy in (*reads[:4], *loads, *reads[4:]):
+    for copy in (*reads[:8], *loads, *reads[8:]):
         copy.start()
-    for k in range(4):
+    for k in range(12):
         reads[k].wait()
         writes[k].start()
     for copy in loads:
@@ -587,7 +590,7 @@
     stores = [pltpu.make_async_copy(results[k], outs[k], out_sems.at[k]) for k in range(6)]
     for copy in stores:
         copy.start()
-    for k in range(4, 16):
+    for k in range(12, 16):
         reads[k].wait()
         writes[k].start()
     for copy in (*writes, *stores):

time: 105 us -> 106 us (level)
  no operation moved by 1% of the time
where the time goes in v5:
time: 106 us; the launch traced here: 105 us
  Pallas kernels  105 us (99%)
    pallas_call x1, Pallas kernels, on_device(): pl.pallas_call(kernel, out_shape=(jax.ShapeDtypeStruct(activations.shape,...  96.7 us
    pallas_call x1, Pallas kernels, on_device(): pl.pallas_call(second_kernel, out_shape=[jax.ShapeDtypeStruct(activations...  8.09 us

profile of v5, /device:TPU:1, one launch (start us, length us, event | category | flops | bytes accessed | tf_op | source)
XLA Modules:
  0.0 105.5 jit_solution(8532602459177341689)
XLA Ops:
  0.6 96.7 %shard_map.162 = (bf16[8192,512]{1,0:T(8,128)(2,1)}, f32[2,64,512]{2,1,0:T(8,128)}, f32[64,128]{1,0:T(8,128)}) custom-call(s32[16]{0:T(128)} %count_ref.1, s32[16]{0:T(128)} %language_ref.1, bf16[8192,512]{1,0:T(8,128)(2,1)} %acts_hbm.1, bf16[512,1024]{1,0:T(8,128)(2,1)} %grad_hbm.1, bf16[512,1024]{1,0:T(8,128)(2,1)} %base_hbm.1, f32[2,64,512]{2,1,0:T(8,128)} %bitcast.6, ...), custom_call_target="tpu_custom_call" | custom-call | flops 25769803776 | bytes 41943040 | tf_op jit(solution)/shard_map/pallas_call | solution.py:617
  97.4 8.1 %shard_map.163 = (bf16[8192,512]{1,0:T(8,128)(2,1)}, f32[2,64,512]{2,1,0:T(8,128)}, f32[2,64,512]{2,1,0:T(8,128)}, f32[2,64,512]{2,1,0:T(8,128)}, f32[2,64,64]{2...) custom-call(bf16[8192,512]{1,0:T(8,128)(2,1)} %get-tuple-element.17.first_hbm, ...), custom_call_target="tpu_custom_call" | custom-call | flops 1048576 | bytes 20971520 | tf_op jit(solution)/shard_map/pallas_call | solution.py:679
